TPU v7x, 256 devices: a whole 4x4x8 slice. The times are simulated.
256 devices in a mesh: ctx: 64 (over z, x, core), dp: 4 (over y).
Axes of the slice: x: 4, y: 4, z: 8, core: 2. Of those that a mesh axis runs over, the one named last changes fastest.
Arguments:
- query_in: bfloat16 [4, 16384, 4096], P('dp', 'ctx'), may hold values from -6 to 6
- key_in: bfloat16 [4, 16384, 512], P('dp', 'ctx'), may hold values from -6 to 6
- value_rows_input: bfloat16 [4, 16384, 512], P('dp', 'ctx'), may hold values from -6 to 6
- grad_out: bfloat16 [4, 16384, 4096], P('dp', 'ctx'), may hold values from -12 to 12
- query_bias: float32 [4096], replicated, may hold values from -1.5 to 1.5
- key_blocks: int32 [4, 128, 6], P('dp'), may hold values from -1 to 127, as said below
- trace_len: int32 [4], P('dp'), may hold values from 8192 to 16384, as said below
Outputs:
- grad_query: bfloat16 [4, 16384, 4096], P('dp', 'ctx')
- grad_key: bfloat16 [4, 16384, 512], P('dp', 'ctx')
- grad_value: bfloat16 [4, 16384, 512], P('dp', 'ctx')
- bias_grad: float32 [4096], replicated
Inputs may be any that keep to these rules, and one draw needn't show every extreme that they name: `key_blocks`: blocks are numbered by position. Entry 2 + d of query block q's list is q - d or -1, and entry 2 is always q; entry r < 2 is r or -1, and -1 whenever r >= q - 3. `trace_len`: some trace has 16384 tokens and some 16384 // 2.
All inputs are finite; a program needn't handle non-finite values.
Results may differ from a plain program's by a relative error of at most 0.011.
The roundings to bfloat16 on the way count: a program that leaves them out, or rounds other values in their place, can miss the bound.
Values may be sent and summed in bfloat16 or wider, within the bound.
A program may use at most 128 MiB of HBM per device.

v0:
```python
import math

import jax
import jax.numpy as jnp
from jax import lax
from jax.sharding import PartitionSpec as P

HEAD_SIZE = 128
BLOCK = 128
PROMPT = 2
WINDOW = 3


def from_behind(value, axis, steps):
    count = lax.axis_size(axis)
    initial, last = (max(0, -steps), min(count, count - steps))
    return lax.ppermute(value, axis, [(source, source + steps) for source in range(initial, last)])


def broadcast(value, axis, source):
    kept = jnp.where(lax.axis_index(axis) == source, value, 0).astype(value.dtype)
    return lax.psum(kept, axis)


def attend(queries, cand_keys, cand_vals, grad_rows, allowed):
    score_scale = HEAD_SIZE ** (-0.5)
    scores = score_scale * jnp.einsum(
        "tqkgd,tskd->tkgqs", queries, cand_keys, preferred_element_type=jnp.float32
    )
    mask_full = allowed[:, None, None]
    scores = jnp.where(mask_full, scores, -1e30)
    row_max = jnp.max(scores, axis=-1, keepdims=True)
    probs = jnp.where(mask_full, jnp.exp(scores - row_max), 0.0)
    totals = jnp.sum(probs, axis=-1, keepdims=True)
    row_live = jnp.any(allowed, axis=-1)[:, None, None, :, None]
    probs = probs / jnp.where(row_live, totals, 1.0)
    probs_low = probs.astype(jnp.bfloat16)
    attended = jnp.einsum(
        "tkgqs,tskd->tqkgd", probs_low, cand_vals, preferred_element_type=jnp.float32
    )
    row_dot = jnp.sum(grad_rows * attended, axis=-1).transpose(0, 2, 3, 1)[..., None]
    grad_probs = jnp.einsum(
        "tqkgd,tskd->tkgqs", grad_rows, cand_vals, preferred_element_type=jnp.float32
    )
    grad_scores = (probs * (grad_probs - row_dot)).astype(jnp.bfloat16)
    grad_query = score_scale * jnp.einsum(
        "tkgqs,tskd->tqkgd", grad_scores, cand_keys, preferred_element_type=jnp.float32
    )
    grad_key = score_scale * jnp.einsum(
        "tkgqs,tqkgd->tskd", grad_scores, queries, preferred_element_type=jnp.float32
    )
    grad_value = jnp.einsum(
        "tkgqs,tqkgd->tskd", probs_low, grad_rows, preferred_element_type=jnp.float32
    )
    return (grad_query, grad_key, grad_value)


def body(query_in, key_in, value_rows_input, grad_out, query_bias, key_blocks, trace_len):
    ctx_count = lax.axis_size("ctx")
    rank_ctx = lax.axis_index("ctx")
    traces = query_in.shape[0]
    width_kv = key_in.shape[-1]
    width_q = query_in.shape[-1]
    heads_kv = width_kv // HEAD_SIZE
    group_size = width_q // width_kv
    cand_count = PROMPT + WINDOW + 1
    kv_pair = jnp.concatenate([key_in, value_rows_input], axis=-1).reshape(
        traces, 2, BLOCK, 2 * width_kv
    )
    own_ids = jnp.stack([rank_ctx, 2 * ctx_count - 1 - rank_ctx])
    half_count = kv_pair.shape[1]
    from_lower = jnp.stack([from_behind(kv_pair, "ctx", offset) for offset in range(1, WINDOW + 1)])
    from_upper = jnp.stack(
        [from_behind(kv_pair, "ctx", -offset) for offset in range(1, WINDOW + 1)]
    )
    offsets = jnp.arange(1, WINDOW + 1, dtype=jnp.int32)
    lower_dev = rank_ctx - offsets
    upper_dev = rank_ctx + offsets
    lower_ids = jnp.stack([lower_dev, 2 * ctx_count - 1 - lower_dev], axis=1)
    upper_ids = jnp.stack([upper_dev, 2 * ctx_count - 1 - upper_dev], axis=1)
    lower_ids = jnp.where((lower_dev >= 0)[:, None], lower_ids, -1000).reshape(-1)
    upper_ids = jnp.where((upper_dev < ctx_count)[:, None], upper_ids, -1000).reshape(-1)
    lower_data = from_lower.transpose(1, 0, 2, 3, 4).reshape(
        traces, WINDOW * half_count, BLOCK, 2 * width_kv
    )
    upper_data = from_upper.transpose(1, 0, 2, 3, 4).reshape(
        traces, WINDOW * half_count, BLOCK, 2 * width_kv
    )
    data_list = [kv_pair, lower_data, upper_data]
    id_list = [own_ids, lower_ids, upper_ids]
    slot_data = jnp.concatenate(data_list, axis=1)
    slot_ids = jnp.concatenate(id_list)
    targets = own_ids[:, None] - jnp.arange(WINDOW + 1, dtype=jnp.int32)[None]
    chooser = (slot_ids[None, None, :] == targets[..., None]).astype(jnp.bfloat16)
    window_kv = jnp.einsum(
        "jdn,tnbf->tjdbf", chooser, slot_data, preferred_element_type=jnp.float32
    ).astype(jnp.bfloat16)
    first_half = kv_pair[:, 0]
    prompt_kv = jnp.stack(
        [broadcast(first_half, "ctx", source) for source in range(PROMPT)], axis=1
    )
    block_rows = jnp.take(key_blocks, own_ids, axis=1)
    queries = (
        (query_in.astype(jnp.float32) + query_bias)
        .astype(jnp.bfloat16)
        .reshape(traces, 2, BLOCK, heads_kv, group_size, HEAD_SIZE)
    )
    grad_rows = grad_out.reshape(traces, 2, BLOCK, heads_kv, group_size, HEAD_SIZE)
    prompt_grad = jnp.zeros((traces, PROMPT, BLOCK, 2 * width_kv), jnp.float32)
    slot_grad = jnp.zeros((traces, slot_data.shape[1], BLOCK, 2 * width_kv), jnp.float32)
    query_parts = []
    for half_idx in range(2):
        block_here = own_ids[half_idx]
        candidates = jnp.concatenate([prompt_kv, window_kv[:, half_idx]], axis=1)
        cand_keys = candidates[..., :width_kv].reshape(
            traces, cand_count * BLOCK, heads_kv, HEAD_SIZE
        )
        cand_vals = candidates[..., width_kv:].reshape(
            traces, cand_count * BLOCK, heads_kv, HEAD_SIZE
        )
        key_ids = jnp.concatenate(
            [
                jnp.arange(PROMPT, dtype=jnp.int32),
                block_here - jnp.arange(WINDOW + 1, dtype=jnp.int32),
            ]
        )
        prompt_ok = jnp.concatenate(
            [
                jnp.arange(PROMPT, dtype=jnp.int32) < block_here - WINDOW,
                jnp.ones((WINDOW + 1,), jnp.bool_),
            ]
        )
        block_ok = (block_rows[:, half_idx] >= 0) & prompt_ok[None]
        key_pos = (key_ids[:, None] * BLOCK + jnp.arange(BLOCK, dtype=jnp.int32)[None]).reshape(-1)
        query_pos = block_here * BLOCK + jnp.arange(BLOCK, dtype=jnp.int32)
        length = trace_len[:, None, None]
        allowed = (
            jnp.repeat(block_ok, BLOCK, axis=1)[:, None, :]
            & (key_pos[None, None, :] <= query_pos[None, :, None])
            & (key_pos[None, None, :] < length)
            & (query_pos[None, :, None] < length)
        )
        grad_query, grad_key, grad_value = attend(
            queries[:, half_idx], cand_keys, cand_vals, grad_rows[:, half_idx], allowed
        )
        query_parts.append(grad_query)
        contrib = jnp.concatenate(
            [
                grad_key.reshape(traces, cand_count, BLOCK, width_kv),
                grad_value.reshape(traces, cand_count, BLOCK, width_kv),
            ],
            axis=-1,
        )
        prompt_grad = prompt_grad + contrib[:, :PROMPT]
        slot_grad = slot_grad + jnp.einsum(
            "dn,tdbf->tnbf",
            chooser[half_idx].astype(jnp.float32),
            contrib[:, PROMPT:],
            precision=lax.Precision.HIGHEST,
        )
    span = WINDOW * half_count
    own_grad = slot_grad[:, 0:2]
    lower_grad = (
        slot_grad[:, 2 : 2 + span]
        .reshape(traces, WINDOW, half_count, BLOCK, 2 * width_kv)
        .transpose(1, 0, 2, 3, 4)
    )
    upper_grad = (
        slot_grad[:, 2 + span : 2 + 2 * span]
        .reshape(traces, WINDOW, half_count, BLOCK, 2 * width_kv)
        .transpose(1, 0, 2, 3, 4)
    )
    low_part = jnp.zeros_like(lower_grad[0])
    up_part = jnp.zeros_like(upper_grad[0])
    for offset in range(1, WINDOW + 1):
        low_part = low_part + from_behind(lower_grad[offset - 1], "ctx", -offset)
        up_part = up_part + from_behind(upper_grad[offset - 1], "ctx", offset)
    kv_grad = own_grad + low_part + up_part
    owners = jnp.arange(PROMPT, dtype=jnp.int32)
    query_all = jnp.stack(query_parts, axis=1)
    local_bias = jnp.sum(query_all, axis=(0, 1, 2)).reshape(width_q)
    shared_total = lax.psum(prompt_grad, "ctx")
    bias_total = lax.psum(local_bias, ("ctx", "dp"))
    owned = (owners == rank_ctx).astype(jnp.float32)
    kv_grad = kv_grad.at[:, 0].add(jnp.sum(owned[None, :, None, None] * shared_total, axis=1))
    grad_query_out = query_all.reshape(traces, 2 * BLOCK, width_q).astype(jnp.bfloat16)
    grad_key_out = kv_grad[..., :width_kv].reshape(traces, 2 * BLOCK, width_kv).astype(jnp.bfloat16)
    grad_value_out = (
        kv_grad[..., width_kv:].reshape(traces, 2 * BLOCK, width_kv).astype(jnp.bfloat16)
    )
    all_traces = traces * lax.axis_size("dp")
    bias_out = bias_total / math.sqrt(all_traces * 2 * BLOCK * ctx_count)
    return (grad_query_out, grad_key_out, grad_value_out, bias_out)


def solution(mesh):
    return jax.shard_map(
        body,
        mesh=mesh,
        in_specs=(
            P("dp", "ctx", None),
            P("dp", "ctx", None),
            P("dp", "ctx", None),
            P("dp", "ctx", None),
            P(),
            P("dp", None, None),
            P("dp"),
        ),
        out_specs=(P("dp", "ctx", None), P("dp", "ctx", None), P("dp", "ctx", None), P()),
        check_vma=False,
    )
```

profile of v0, /device:TPU:1, one launch (start us, length us, event | category | flops | bytes accessed | tf_op | source)
XLA Modules:
  0.0 587.6 jit_solution(5824512596889643687)
XLA Ops:
  11.0 5.2 collective-permute-start.3
  16.2 7.4 %collective-permute-start.2 = (bf16[1,2,128,1024]{3,2,1,0:T(8,128)(2,1)S(1)}, bf16[1,2,128,1024]{3,2,1,0:T(8,128)(2,1)}, u32[]{:S(2)}, u32[]{:S(2)}) collective-permute-start(bf16[1,2,128,1024]{3,2,1,0:T(8,128)(2,1)S(1)} %bitcast.330), channel_id=1, source_target_pairs={{0,12},{4,16},{8,20},{12,24},{16,28},{20,32},{24,36},{28,40},{32,4... | collective-permute-start | bytes 1572872 | tf_op jit(solution)/shard_map/ppermute | solution.py:17
  23.6 2.7 collective-permute-start.1
  38.9 2.9 fusion.73
  44.5 3.3 fusion.74
  50.2 3.2 collective-permute-done
  55.7 2.7 convert_bitcast_fusion
  60.2 161.4 %all-reduce.8.cloned.1.call-done = (bf16[1,1,128,1024]{3,1,2,0:T(2,128)(2,1)}, bf16[1,1,128,1024]{3,1,2,0:T(2,128)(2,1)}) async-done(((bf16[1,1,128,1024]{3,1,2,0:T(2,128)(2,1)}, bf16[1,1,128,1024]{3,1,2,0:T(2,128)(2,1)}), (bf16[1,1,128,1024]{3,1,2,0:T(2,128)(2,1)}, bf16[1,1,128,1024]{3,1,2,0:T(2,128)(2,1)})) %all-reduce.8.cloned.1.call-update) | async-done | bytes 524304 | tf_op jit(solution)/shard_map/psum | solution.py:22
  221.6 4.6 pad_maximum_fusion
  232.6 2.7 fusion.75
  247.8 3.2 fusion.9
  251.1 5.3 fusion.40
  256.4 5.2 fusion.29
  261.6 7.1 %fusion.11 = bf16[4,8,128,768]{2,3,1,0:T(8,128)(2,1)S(1)} fusion(f32[4,8,128]{2,1,0:T(8,128)S(1)} %bitcast.338, f32[4,8,128]{2,1,0:T(8,128)S(1)} %broadcast_select_fusion.2, f32[4,8,128]{2,1,0:T(8,128)S(1)} %get-tuple-element.46, f32[4,768,128,8]{2,1,3,0:T(8,128)S(1)} %get-tuple-element.47, pred[128,768]{0,1:T(8,128)(4,1)S(1)} %and_and_fusion, ...), kind=kOutput, calls=%fused_computation.19 | convolution fusion | flops 830472192 | bytes 20856832 | tf_op jit(solution)/shard_map/tqkgd,tskd->tkgqs/dot_general | solution.py:42
  271.8 3.4 fusion.35
  275.2 2.8 copy.106
  278.0 3.7 copy_dynamic-update-slice_fusion.1
  284.1 3.2 fusion.7
  287.4 4.8 fusion.37
  292.2 5.2 fusion.30
  297.4 7.3 %fusion.10 = bf16[4,8,128,768]{2,3,1,0:T(8,128)(2,1)S(1)} fusion(f32[4,8,128]{2,1,0:T(8,128)S(1)} %bitcast.339, f32[4,8,128]{2,1,0:T(8,128)S(1)} %broadcast_select_fusion.3, f32[4,8,128]{2,1,0:T(8,128)S(1)} %get-tuple-element.48, f32[4,768,128,8]{2,1,3,0:T(8,128)S(1)} %get-tuple-element.49, pred[128,768]{0,1:T(8,128)(4,1)S(1)} %and_and_fusion.1, ...), kind=kOutput, calls=%fused_computation.18 | convolution fusion | flops 830472192 | bytes 20856832 | tf_op jit(solution)/shard_map/tqkgd,tskd->tkgqs/dot_general | solution.py:42
  307.8 3.4 fusion.36
  317.3 6.9 %fusion.28 = f32[128,1024,14]{1,2,0:T(8,128)} fusion(f32[1,6,128,1024]{3,1,2,0:T(8,128)S(1)} %copy_dynamic-update-slice_fusion.2, pred[2,4,14]{2,1,0:T(4,128)(4,1)S(1)} %copy-done.26), kind=kOutput, calls=%fused_computation.40 | convolution fusion | flops 88080384 | bytes 9437696 | tf_op jit(solution)/shard_map/dn,tdbf->tnbf/dot_general | solution.py:155
  329.2 10.6 %add_bitcast_fusion = f32[1,14,128,1024]{3,1,2,0:T(8,128)S(1)} fusion(f32[128,1024,14]{1,2,0:T(8,128)} %fusion.28, f32[1,6,128,1024]{3,1,2,0:T(8,128)} %copy-done.4, pred[2,4,14]{2,1,0:T(4,128)(4,1)S(1)} %copy-done.26), kind=kOutput, calls=%fused_computation.17 | convolution fusion | flops 89915392 | bytes 17826304 | tf_op jit(solution)/shard_map/dn,tdbf->tnbf/dot_general | solution.py:155
  339.8 3.6 fusion.71
  345.9 9.2 %collective-permute-start.11 = (f32[1,2,128,1024]{3,1,2,0:T(2,128)}, f32[1,2,128,1024]{3,1,2,0:T(2,128)}, u32[]{:S(2)}, u32[]{:S(2)}) collective-permute-start(f32[1,2,128,1024]{3,1,2,0:T(2,128)} %get-tuple-element.21), channel_id=1, source_target_pairs={{0,12},{4,16},{8,20},{12,24},{16,28},{20,32},{24,36},{28,40},{32,4... | collective-permute-start | bytes 3145736 | tf_op jit(solution)/shard_map/ppermute | solution.py:17
  366.5 8.7 %collective-permute-done.7 = f32[1,2,128,1024]{3,1,2,0:T(2,128)S(1)} collective-permute-done((f32[1,2,128,1024]{3,1,2,0:T(2,128)S(1)}, f32[1,2,128,1024]{3,1,2,0:T(2,128)S(1)}, u32[]{:S(2)}, u32[]{:S(2)}) %collective-permute-start.7) | collective-permute-done | bytes 1048608 | tf_op jit(solution)/shard_map/ppermute | solution.py:17
  375.2 19.0 %collective-permute-start.6 = (f32[1,2,128,1024]{3,1,2,0:T(2,128)}, f32[1,2,128,1024]{3,1,2,0:T(2,128)}, u32[]{:S(2)}, u32[]{:S(2)}) collective-permute-start(f32[1,2,128,1024]{3,1,2,0:T(2,128)} %get-tuple-element.25), channel_id=1, source_target_pairs={{4,0},{8,4},{12,8},{16,12},{20,16},{24,20},{28,24},{32,28},{36,32}... | collective-permute-start | bytes 3145736 | tf_op jit(solution)/shard_map/ppermute | solution.py:17
  398.4 93.1 %psum.31 = f32[4096]{0:T(1024)S(1)} all-reduce(f32[4096]{0:T(1024)S(1)} %add_bitcast_fusion.1), channel_id=1, replica_groups=mesh['ctx'=64,'dp'=4] {'ctx','dp'}, use_global_device_ids=true, to_apply=%region_14.15 | all-reduce | flops 4096 | bytes 32768 | tf_op jit(solution)/shard_map/psum | solution.py:183
  492.1 73.7 %all-reduce.6.cloned.1.call-done = f32[1,2,128,1024]{3,1,2,0:T(2,128)} async-done(((f32[1,2,128,1024]{3,1,2,0:T(2,128)}), f32[1,2,128,1024]{3,1,2,0:T(2,128)}) %all-reduce.6.cloned.1.call-update) | async-done | bytes 1048592 | tf_op jit(solution)/shard_map/psum | solution.py:182
  568.5 5.6 fusion.45
  574.6 3.7 scatter-add.4
  (170 shorter events, 87.0 us)
Async XLA Ops:
  7.2 24.0 %copy-start.13 = (bf16[1,256,4096]{2,1,0:T(8,128)(2,1)S(1)}, bf16[1,256,4096]{2,1,0:T(8,128)(2,1)}, u32[]{:S(2)}) copy-start(bf16[1,256,4096]{2,1,0:T(8,128)(2,1)} %param.9) | copy-start | bytes 6291460
  7.2 214.4 %all-reduce.8.cloned.1.call-start = ((), (), s32[]{:S(2)}) async-start(), calls=%async_computation.1 | async-start | bytes 2097152 | tf_op jit(solution)/shard_map/psum | solution.py:22
  8.4 33.6 %collective-permute-start.5 = (bf16[1,2,128,1024]{3,2,1,0:T(8,128)(2,1)S(1)}, bf16[1,2,128,1024]{3,2,1,0:T(8,128)(2,1)}, u32[]{:S(2)}, u32[]{:S(2)}) collective-permute-start(bf16[1,2,128,1024]{3,2,1,0:T(8,128)(2,1)S(1)} %bitcast.327), channel_id=1, source_target_pairs={{12,0},{16,4},{20,8},{24,12},{28,16},{32,20},{36,24},{40,28},{44,3... | collective-permute-start | bytes 1572872 | tf_op jit(solution)/shard_map/ppermute | solution.py:17
  9.7 38.0 %collective-permute-start.4 = (bf16[1,2,128,1024]{3,2,1,0:T(8,128)(2,1)S(1)}, bf16[1,2,128,1024]{3,2,1,0:T(8,128)(2,1)}, u32[]{:S(2)}, u32[]{:S(2)}) collective-permute-start(bf16[1,2,128,1024]{3,2,1,0:T(8,128)(2,1)S(1)} %bitcast.328), channel_id=1, source_target_pairs={{8,0},{12,4},{16,8},{20,12},{24,16},{28,20},{32,24},{36,28},{40,32... | collective-permute-start | bytes 1572872 | tf_op jit(solution)/shard_map/ppermute | solution.py:17
  11.0 36.7 %collective-permute-start.3 = (bf16[1,2,128,1024]{3,2,1,0:T(8,128)(2,1)S(1)}, bf16[1,2,128,1024]{3,2,1,0:T(8,128)(2,1)}, u32[]{:S(2)}, u32[]{:S(2)}) collective-permute-start(bf16[1,2,128,1024]{3,2,1,0:T(8,128)(2,1)S(1)} %bitcast.329), channel_id=1, source_target_pairs={{4,0},{8,4},{12,8},{16,12},{20,16},{24,20},{28,24},{32,28},{36,32}... | collective-permute-start | bytes 1572872 | tf_op jit(solution)/shard_map/ppermute | solution.py:17
  16.2 34.0 %collective-permute-start.2 = (bf16[1,2,128,1024]{3,2,1,0:T(8,128)(2,1)S(1)}, bf16[1,2,128,1024]{3,2,1,0:T(8,128)(2,1)}, u32[]{:S(2)}, u32[]{:S(2)}) collective-permute-start(bf16[1,2,128,1024]{3,2,1,0:T(8,128)(2,1)S(1)} %bitcast.330), channel_id=1, source_target_pairs={{0,12},{4,16},{8,20},{12,24},{16,28},{20,32},{24,36},{28,40},{32,4... | collective-permute-start | bytes 1572872 | tf_op jit(solution)/shard_map/ppermute | solution.py:17
  23.6 26.6 %collective-permute-start.1 = (bf16[1,2,128,1024]{3,2,1,0:T(8,128)(2,1)S(1)}, bf16[1,2,128,1024]{3,2,1,0:T(8,128)(2,1)}, u32[]{:S(2)}, u32[]{:S(2)}) collective-permute-start(bf16[1,2,128,1024]{3,2,1,0:T(8,128)(2,1)S(1)} %bitcast.331), channel_id=1, source_target_pairs={{0,8},{4,12},{8,16},{12,20},{16,24},{20,28},{24,32},{28,36},{32,40... | collective-permute-start | bytes 1572872 | tf_op jit(solution)/shard_map/ppermute | solution.py:17
  28.7 537.1 %all-reduce.6.cloned.1.call-start = ((), (), s32[]{:S(2)}) async-start(), calls=%async_computation | async-start | bytes 2097152 | tf_op jit(solution)/shard_map/psum | solution.py:182
  36.5 19.2 %copy-start.25 = (pred[2,4,14]{2,1,0:T(4,128)(4,1)}, pred[2,4,14]{2,1,0:T(4,128)(4,1)S(1)}, u32[]{:S(2)}) copy-start(pred[2,4,14]{2,1,0:T(4,128)(4,1)S(1)} %broadcast_compare_fusion.2) | copy-start | bytes 340
  41.8 203.6 %copy-start.9 = (bf16[1,1,128,4,8,128]{5,4,3,2,1,0:T(8,128)(2,1)}, bf16[1,1,128,4,8,128]{5,4,3,2,1,0:T(8,128)(2,1)S(1)}, u32[]{:S(2)}) copy-start(bf16[1,1,128,4,8,128]{5,4,3,2,1,0:T(8,128)(2,1)S(1)} %get-tuple-element.29) | copy-start | bytes 3145732
  42.1 11.4 %collective-permute-start = (bf16[1,2,128,1024]{3,2,1,0:T(8,128)(2,1)S(1)}, bf16[1,2,128,1024]{3,2,1,0:T(8,128)(2,1)S(1)}, u32[]{:S(2)}, u32[]{:S(2)}) collective-permute-start(bf16[1,2,128,1024]{3,2,1,0:T(8,128)(2,1)S(1)} %bitcast.333), channel_id=1, source_target_pairs={{0,4},{4,8},{8,12},{12,16},{16,20},{20,24},{24,28},{28,32},{32,36}... | collective-permute-start | bytes 1572872 | tf_op jit(solution)/shard_map/ppermute | solution.py:17
  238.1 9.7 %copy-start.5 = (bf16[768,4,128]{2,1,0:T(4,128)(2,1)}, bf16[768,4,128]{2,1,0:T(4,128)(2,1)S(1)}, u32[]{:S(2)}) copy-start(bf16[768,4,128]{2,1,0:T(4,128)(2,1)S(1)} %reshape.1055) | copy-start | bytes 2359300
  261.6 7.1 %copy-start.15 = (f32[1,768,4,128]{3,1,2,0:T(8,128)S(1)}, f32[1,768,4,128]{3,1,2,0:T(8,128)}, u32[]{:S(2)}) copy-start(f32[1,768,4,128]{3,1,2,0:T(8,128)} %fusion.40) | copy-start | bytes 4718596
  261.6 10.2 %copy-start.10 = (bf16[1,1,128,4,8,128]{5,4,3,2,1,0:T(8,128)(2,1)S(1)}, bf16[1,1,128,4,8,128]{5,4,3,2,1,0:T(8,128)(2,1)}, u32[]{:S(2)}) copy-start(bf16[1,1,128,4,8,128]{5,4,3,2,1,0:T(8,128)(2,1)} %copy-done.9) | copy-start | bytes 3145732
  275.2 6.6 %copy-start.7 = (bf16[1,1,128,4,8,128]{5,4,3,2,1,0:T(8,128)(2,1)S(1)}, bf16[1,1,128,4,8,128]{5,4,3,2,1,0:T(8,128)(2,1)}, u32[]{:S(2)}) copy-start(bf16[1,1,128,4,8,128]{5,4,3,2,1,0:T(8,128)(2,1)} %get-tuple-element.28) | copy-start | bytes 3145732
  297.4 7.3 %copy-start.16 = (f32[1,768,4,128]{3,1,2,0:T(8,128)S(1)}, f32[1,768,4,128]{3,1,2,0:T(8,128)}, u32[]{:S(2)}) copy-start(f32[1,768,4,128]{3,1,2,0:T(8,128)} %fusion.37) | copy-start | bytes 4718596
  297.4 10.5 %copy-start.8 = (bf16[1,1,128,4,8,128]{5,4,3,2,1,0:T(8,128)(2,1)S(1)}, bf16[1,1,128,4,8,128]{5,4,3,2,1,0:T(8,128)(2,1)}, u32[]{:S(2)}) copy-start(bf16[1,1,128,4,8,128]{5,4,3,2,1,0:T(8,128)(2,1)} %get-tuple-element.28) | copy-start | bytes 3145732
  311.2 6.0 %copy-start.26 = (pred[2,4,14]{2,1,0:T(4,128)(4,1)S(1)}, pred[2,4,14]{2,1,0:T(4,128)(4,1)}, u32[]{:S(2)}) copy-start(pred[2,4,14]{2,1,0:T(4,128)(4,1)} %copy-done.25) | copy-start | bytes 340
  317.2 6.9 %copy-start.3 = (f32[1,6,128,1024]{3,1,2,0:T(8,128)S(1)}, f32[1,6,128,1024]{3,1,2,0:T(8,128)}, u32[]{:S(2)}) copy-start(f32[1,6,128,1024]{3,1,2,0:T(8,128)} %copy_dynamic-update-slice_fusion.1) | copy-start | bytes 9437188
  317.3 6.9 %copy-start.11 = (f32[1,768,4,128]{3,2,0,1:T(4,128)S(1)}, f32[1,768,4,128]{3,2,0,1:T(4,128)}, u32[]{:S(2)}) copy-start(f32[1,768,4,128]{3,2,0,1:T(4,128)} %copy.107) | copy-start | bytes 4718596
  327.1 34.3 %slice-start = ((s8[6291456]{0:T(1024)(128)(4,1)}), s8[2097152]{0:T(1024)(128)(4,1)S(1)}, s32[]{:S(2)}) async-start(s8[6291456]{0:T(1024)(128)(4,1)} %bitcast.308), calls=%async_computation.2 | async-start | bytes 4194304
  329.2 32.3 %slice-start.1 = ((s8[6291456]{0:T(1024)(128)(4,1)}), s8[4194304]{0:T(1024)(128)(4,1)S(1)}, s32[]{:S(2)}) async-start(s8[6291456]{0:T(1024)(128)(4,1)} %bitcast.308), calls=%async_computation.3 | async-start | bytes 8388608
  339.8 21.6 %copy-start.6 = (bf16[768,4,128]{2,1,0:T(4,128)(2,1)S(1)}, bf16[768,4,128]{2,1,0:T(4,128)(2,1)}, u32[]{:S(2)}) copy-start(bf16[768,4,128]{2,1,0:T(4,128)(2,1)} %copy-done.5) | copy-start | bytes 2359300
  344.7 30.6 %collective-permute-start.7 = (f32[1,2,128,1024]{3,1,2,0:T(2,128)S(1)}, f32[1,2,128,1024]{3,1,2,0:T(2,128)S(1)}, u32[]{:S(2)}, u32[]{:S(2)}) collective-permute-start(f32[1,2,128,1024]{3,1,2,0:T(2,128)S(1)} %get-tuple-element.20), channel_id=1, source_target_pairs={{8,0},{12,4},{16,8},{20,12},{24,16},{28,20},{32,24},{36,28},{40,32... | collective-permute-start | bytes 3145736 | tf_op jit(solution)/shard_map/ppermute | solution.py:17
  345.9 222.5 %collective-permute-start.11 = (f32[1,2,128,1024]{3,1,2,0:T(2,128)}, f32[1,2,128,1024]{3,1,2,0:T(2,128)}, u32[]{:S(2)}, u32[]{:S(2)}) collective-permute-start(f32[1,2,128,1024]{3,1,2,0:T(2,128)} %get-tuple-element.21), channel_id=1, source_target_pairs={{0,12},{4,16},{8,20},{12,24},{16,28},{20,32},{24,36},{28,40},{32,4... | collective-permute-start | bytes 3145736 | tf_op jit(solution)/shard_map/ppermute | solution.py:17
  355.2 213.3 %collective-permute-start.10 = (f32[1,2,128,1024]{3,1,2,0:T(2,128)}, f32[1,2,128,1024]{3,1,2,0:T(2,128)}, u32[]{:S(2)}, u32[]{:S(2)}) collective-permute-start(f32[1,2,128,1024]{3,1,2,0:T(2,128)} %get-tuple-element.22), channel_id=1, source_target_pairs={{0,8},{4,12},{8,16},{12,20},{16,24},{20,28},{24,32},{28,36},{32,40... | collective-permute-start | bytes 3145736 | tf_op jit(solution)/shard_map/ppermute | solution.py:17
  357.4 211.0 %collective-permute-start.9 = (f32[1,2,128,1024]{3,1,2,0:T(2,128)}, f32[1,2,128,1024]{3,1,2,0:T(2,128)}, u32[]{:S(2)}, u32[]{:S(2)}) collective-permute-start(f32[1,2,128,1024]{3,1,2,0:T(2,128)} %get-tuple-element.23), channel_id=1, source_target_pairs={{0,4},{4,8},{8,12},{12,16},{16,20},{20,24},{24,28},{28,32},{32,36}... | collective-permute-start | bytes 3145736 | tf_op jit(solution)/shard_map/ppermute | solution.py:17
  359.4 209.1 %collective-permute-start.8 = (f32[1,2,128,1024]{3,1,2,0:T(2,128)}, f32[1,2,128,1024]{3,1,2,0:T(2,128)}, u32[]{:S(2)}, u32[]{:S(2)}) collective-permute-start(f32[1,2,128,1024]{3,1,2,0:T(2,128)} %get-tuple-element.24), channel_id=1, source_target_pairs={{12,0},{16,4},{20,8},{24,12},{28,16},{32,20},{36,24},{40,28},{44,3... | collective-permute-start | bytes 3145736 | tf_op jit(solution)/shard_map/ppermute | solution.py:17
  375.2 19.5 %copy-start.21 = (f32[1,2,128,1024]{3,1,2,0:T(2,128)}, f32[1,2,128,1024]{3,1,2,0:T(2,128)S(1)}, u32[]{:S(2)}) copy-start(f32[1,2,128,1024]{3,1,2,0:T(2,128)S(1)} %collective-permute-done.7) | copy-start | bytes 3145732
  375.2 193.2 %collective-permute-start.6 = (f32[1,2,128,1024]{3,1,2,0:T(2,128)}, f32[1,2,128,1024]{3,1,2,0:T(2,128)}, u32[]{:S(2)}, u32[]{:S(2)}) collective-permute-start(f32[1,2,128,1024]{3,1,2,0:T(2,128)} %get-tuple-element.25), channel_id=1, source_target_pairs={{4,0},{8,4},{12,8},{16,12},{20,16},{24,20},{28,24},{32,28},{36,32}... | collective-permute-start | bytes 3145736 | tf_op jit(solution)/shard_map/ppermute | solution.py:17
  394.5 171.3 %copy-start.27 = (f32[2]{0:T(128)S(1)}, f32[2]{0:T(128)}, u32[]{:S(2)}) copy-start(f32[2]{0:T(128)} %compare_convert_fusion) | copy-start | bytes 28
  396.1 172.4 %copy-start.22 = (f32[1,2,128,1024]{3,1,2,0:T(2,128)S(1)}, f32[1,2,128,1024]{3,1,2,0:T(2,128)}, u32[]{:S(2)}) copy-start(f32[1,2,128,1024]{3,1,2,0:T(2,128)} %copy-done.21) | copy-start | bytes 3145732
  (14 other events, 58.0 us)
Sparse Core Ops, SparseCore 0:
  28.8 192.6 all-reduce.7
  329.3 236.4 all-reduce.5
where the time goes:
time: 595 us; the launch traced here: 588 us
  waiting for transfers between devices  247 us (42%)
  blocking collectives  93.1 us (16%)
  matrix products  71.3 us (12%)
  local copies, waits for them, and re-layouts  70.5 us (12%)
  starting transfers between devices  55.6 us (9%)
  other arithmetic  34.3 us (6%)
  between operations  15.7 us (3%)
    psum x1, waiting for transfers between devices, broadcast(): return lax.psum(kept, axis)  161 us
    psum x1, blocking collectives, body(): bias_total = lax.psum(local_bias, ('ctx', 'dp'))  93.1 us
    psum x1, waiting for transfers between devices, body(): shared_total = lax.psum(prompt_grad, 'ctx')  73.7 us
    ppermute x12, starting transfers between devices, from_behind(): lax.ppermute(value, axis, [(source, source + steps) for source in range(i...  55.5 us
    dot_general x2, matrix products, body(): jnp.einsum('dn,tdbf->tnbf', chooser[half_idx].astype(jnp.float32), contri...  17.5 us
    unnamed x69, local copies, waits for them, and re-layouts  14.9 us
    dot_general x2, matrix products, attend(): jnp.einsum('tqkgd,tskd->tkgqs', grad_rows, cand_vals, preferred_element_t...  14.4 us
    ppermute x12, waiting for transfers between devices, from_behind(): lax.ppermute(value, axis, [(source, source + steps) for source in range(i...  11.9 us
  transfers between devices with their start and end apart: 14, of which 4 were waited for; matrix products, arithmetic and copies ran while one was open for 9% of the time, Pallas kernels for 0%

commit v1 on v0

v1 whole, which is shorter than its diff:
```python
import math

import jax
import jax.numpy as jnp
from jax import lax
from jax.experimental import pallas as pl
from jax.experimental.pallas import tpu as pltpu
from jax.sharding import PartitionSpec as P

HEAD_SIZE = 128
BLOCK = 128
PROMPT = 2
WINDOW = 3
N_CTX = 64
NZ, NX, NY = 8, 4, 4
GROUPS = 4
PER_GROUP = 8
PIECE = BLOCK // NZ
SLOTS = PROMPT + WINDOW + 1
ROWS = 65536
SCALE = HEAD_SIZE ** (-0.5)
SCALE2 = SCALE * math.log2(math.e)
FAR = -1e30
BF, F32 = jnp.bfloat16, jnp.float32
MESH = pl.DeviceIdType.MESH


def dot(a, b, ca, cb):
    return lax.dot_general(a, b, (((ca,), (cb,)), ((), ())), preferred_element_type=F32)


def kernel(q_hbm, k_hbm, v_hbm, go_hbm, bias_ref, kb_ref, tl_ref,
           dq_ref, dk_ref, dv_ref, db_ref,
           qv, gv, stage, prompt, win, ret_s, ret_r, refl_r, own, pacc, ps, st1, st2s, st2,
           bsrc, b1, b2s, b2, b3s, b3,
           q_sem, g_sem, kv_sem, win_ss, win_rs, s1_ss, s1_rs, s2_ss, s2_rs, s3_ss, s3_rs,
           ret_ss, ret_rs, refl_rs, st1_ss, st1_rs, st2_ss, st2_rs, b1_ss, b1_rs, b2_ss, b2_rs, b3_ss, b3_rs):
    c = lax.axis_index("ctx")
    y = lax.axis_index("dp")
    core = lax.rem(c, 2)
    x = lax.rem(c // 2, NX)
    z = c // (2 * NX)
    gi = z * 2 + core

    def at(zz, xx, rr):
        return (zz * NX + xx) * 2 + rr

    def rcopy(src, dst, ss, rs, dev):
        return pltpu.make_async_remote_copy(src_ref=src, dst_ref=dst, send_sem=ss, recv_sem=rs,
                                            device_id={"ctx": dev}, device_id_type=MESH)

    def ycopy(src, dst, ss, rs, dev):
        return pltpu.make_async_remote_copy(src_ref=src, dst_ref=dst, send_sem=ss, recv_sem=rs,
                                            device_id={"dp": dev}, device_id_type=MESH)

    def wait_bytes(ref, sem):
        pltpu.make_async_copy(ref, ref, sem).wait()

    def loop(lo, hi, f):
        def step(i, carry):
            f(i)
            return carry
        lax.fori_loop(lo, hi, step, 0)

    def kv_load(half, kv, g):
        src = k_hbm if kv == 0 else v_hbm
        return pltpu.make_async_copy(
            src.at[pl.ds(half * BLOCK, BLOCK), pl.ds(pl.multiple_of(g * 128, 128), 128)],
            stage.at[half, g, kv], kv_sem.at[half, kv, g])

    def q_load(src, dst, sem, g):
        return pltpu.make_async_copy(
            src.at[:, pl.ds(pl.multiple_of(g * 1024, 1024), 1024)], dst.at[g], sem.at[g])

    def start_loads(g):
        for half in range(2):
            for kv in range(2):
                kv_load(half, kv, g).start()
    loop(0, GROUPS, start_loads)

    def start_q(g):
        q_load(q_hbm, qv, q_sem, g).start()
        q_load(go_hbm, gv, g_sem, g).start()
    loop(0, GROUPS, start_q)

    barrier = pltpu.get_barrier_semaphore()

    def greet(dev):
        pl.semaphore_signal(barrier, inc=1, device_id={"ctx": dev}, device_id_type=MESH)

    is_root = c < PROMPT

    def zero(g):
        refl_r[g] = jnp.zeros((WINDOW, 2, BLOCK, 128), BF)
        ret_r[1, g] = jnp.zeros((WINDOW, 2, BLOCK, 128), BF)
    loop(0, GROUPS, zero)

    for d in range(1, WINDOW + 1):
        greet(lax.rem(c + d, N_CTX))
        greet(lax.rem(c + N_CTX - d, N_CTX))

    def greet_group(k):
        j = lax.rem(gi + k, 16)
        greet(at(j // 2, x, lax.rem(j, 2)))
    loop(1, 16, greet_group)

    def greet_row(k):
        j = lax.rem(x * 2 + core + k, 8)
        greet(at(z, j // 2, lax.rem(j, 2)))
    loop(1, 8, greet_row)

    def greet_y(k):
        pl.semaphore_signal(barrier, inc=1, device_id={"dp": lax.rem(y + k, NY)}, device_id_type=MESH)
    loop(1, NY, greet_y)

    @pl.when(is_root)
    def _():
        def greet_senders(k):
            greet(k * 2 + core)
        loop(1, NZ * NX, greet_senders)

    def wait_loads(g):
        for half in range(2):
            for kv in range(2):
                kv_load(half, kv, g).wait()
    loop(0, GROUPS, wait_loads)

    @pl.when(is_root)
    def _():
        pl.semaphore_wait(barrier, 31)

    @pl.when(jnp.logical_not(is_root))
    def _():
        pl.semaphore_wait(barrier, 32)

    def piece(g, r, p):
        return prompt.at[g, r, :, pl.ds(pl.multiple_of(p * PIECE, PIECE), PIECE), :]

    @pl.when(is_root)
    def _():
        def own_piece(g):
            prompt[g, core, :, 0:PIECE, :] = stage[0, g, :, 0:PIECE, :]

            def scatter(p):
                rcopy(stage.at[0, g, :, pl.ds(pl.multiple_of(p * PIECE, PIECE), PIECE), :],
                      piece(g, core, p), s1_ss.at[g], s1_rs.at[g], at(p, 0, core)).start()
            loop(1, NZ, scatter)
        loop(0, GROUPS, own_piece)

    def win_low(g, d):
        return rcopy(stage.at[0, g], win.at[0, g, d - 1], win_ss.at[0, g, d - 1], win_rs.at[0, g, d - 1],
                     lax.rem(c + d, N_CTX))

    def win_up(g, d, half, dev):
        return rcopy(stage.at[half, g], win.at[1, g, d - 1], win_ss.at[1 + (half == 0), g, d - 1],
                     win_rs.at[1, g, d - 1], dev)

    def fold(d):
        return N_CTX * 2 - 1 - c - d

    def is_self(d):
        return c == fold(d)

    def send_window(g):
        for d in range(1, WINDOW + 1):
            win_low(g, d).start()

            @pl.when(c >= d)
            def _():
                win_up(g, d, 1, c - d).start()

            @pl.when((c >= N_CTX - d) & jnp.logical_not(is_self(d)))
            def _():
                win_up(g, d, 0, fold(d)).start()
            if d % 2 == 1:
                @pl.when(is_self(d))
                def _():
                    win[1, g, d - 1] = stage[0, g]

    def done_window(g):
        for d in range(1, WINDOW + 1):
            win_low(g, d).wait_send()

            @pl.when(c >= d)
            def _():
                win_up(g, d, 1, c - d).wait_send()

            @pl.when((c >= N_CTX - d) & jnp.logical_not(is_self(d)))
            def _():
                win_up(g, d, 0, fold(d)).wait_send()

    def wait_window(g, b):
        for d in range(1, WINDOW + 1):
            if b == 0:
                win_low(g, d).wait_recv()
            elif d % 2 == 1:
                @pl.when(jnp.logical_not(is_self(d)))
                def _():
                    win_up(g, d, 1, c).wait_recv()
            else:
                win_up(g, d, 1, c).wait_recv()

    def prompt_row(g):
        @pl.when(x == 0)
        def _():
            @pl.when(z > 0)
            def _():
                wait_bytes(piece(g, core, z), s1_rs.at[g])

            def send(k):
                j = lax.rem(core + k, 8)
                rcopy(piece(g, core, z), piece(g, core, z), s2_ss.at[g], s2_rs.at[g, core],
                      at(z, j // 2, lax.rem(j, 2))).start()
            loop(1, 8, send)

    def zpieces(g):
        return prompt.at[g, :, :, pl.ds(pl.multiple_of(z * PIECE, PIECE), PIECE), :]

    def prompt_column(g):
        for r in range(PROMPT):
            @pl.when((x > 0) | (core != r))
            def _():
                wait_bytes(piece(g, r, z), s2_rs.at[g, r])

        def send(k):
            rcopy(zpieces(g), zpieces(g), s3_ss.at[g], s3_rs.at[g], at(lax.rem(z + k, NZ), x, core)).start()
        loop(1, NZ, send)

    def seven(g):
        return prompt.at[g, :, :, pl.ds(0, (NZ - 1) * PIECE), :]

    send_window(0)
    prompt_row(0)
    prompt_row(1)
    prompt_column(0)
    loop(1, GROUPS, send_window)

    kk = lax.broadcasted_iota(jnp.int32, (BLOCK, PER_GROUP * 128), 0)
    qi = lax.rem(lax.broadcasted_iota(jnp.int32, (BLOCK, PER_GROUP * 128), 1), BLOCK)
    lane = lax.rem(lax.broadcasted_iota(jnp.int32, (1, PER_GROUP * 128), 1), BLOCK)
    length = tl_ref[0]

    def unit(g, b):
        blk = c if b == 0 else N_CTX * 2 - 1 - c
        rows = slice(b * BLOCK, (b + 1) * BLOCK)
        bias = bias_ref[pl.ds(pl.multiple_of(g * 8, 8), 8), :]
        Q = jnp.concatenate(
            [(qv[g, rows, j * 128:(j + 1) * 128].astype(F32) + bias[j:j + 1]).astype(BF) for j in range(PER_GROUP)], 0)
        G = jnp.concatenate([gv[g, rows, j * 128:(j + 1) * 128] for j in range(PER_GROUP)], 0)
        K, V = (jnp.concatenate(
            [prompt[g, 0, kv], prompt[g, 1, kv], stage[b, g, kv],
             win[b, g, 0, kv], win[b, g, 1, kv], win[b, g, 2, kv]], 0) for kv in range(2))
        off = [jnp.where(kb_ref[0, blk, s] >= 0, 0.0, FAR).astype(F32) for s in range(SLOTS)]
        S = dot(K, Q, 1, 1)
        parts, m = [], None
        for s in range(SLOTS):
            v = S[s * 128:(s + 1) * 128]
            if s == PROMPT:
                v = jnp.where(kk <= qi, v, FAR)
            parts.append(v)
            mm = jnp.max(v, 0, keepdims=True) + off[s]
            m = mm if m is None else jnp.maximum(m, mm)
        m = m * SCALE2
        exps, tot = [], None
        for s in range(SLOTS):
            p = jnp.exp2(parts[s] * SCALE2 - (m - off[s]))
            exps.append(p)
            t = jnp.sum(p, 0, keepdims=True)
            tot = t if tot is None else tot + t
        inv = jnp.where(blk * BLOCK + lane < length, 1.0 / tot, 0.0)
        probs = jnp.concatenate(exps, 0) * inv
        low = probs.astype(BF)
        dP = dot(V, G, 1, 1)
        r = jnp.sum(low.astype(F32) * dP, 0, keepdims=True)
        dS = (probs * (dP - r)).astype(BF)
        dv = dot(low, G, 1, 0)
        dk = dot(dS, Q, 1, 0) * SCALE
        dqT = dot(K, dS, 0, 0)
        for j in range(PER_GROUP):
            t = dqT[:, j * 128:(j + 1) * 128].T * SCALE
            dq_ref[rows, pl.ds(pl.multiple_of(g * 1024 + j * 128, 128), 128)] = t.astype(BF)
            t = jnp.sum(t, 0, keepdims=True)
            if b == 0:
                bsrc[g, j:j + 1, :] = t
            else:
                bsrc[g, j:j + 1, :] = bsrc[g, j:j + 1, :] + t
        for kv, val in ((0, dk), (1, dv)):
            for s in range(PROMPT):
                w = val[s * 128:(s + 1) * 128]
                if b == 0:
                    pacc[s, kv] = w
                else:
                    ps[g, s, kv] = (pacc[s, kv] + w).astype(BF)
            own[b, g, kv] = val[256:384]
            for d in range(WINDOW):
                ret_s[b, g, d, kv] = val[384 + d * 128:512 + d * 128].astype(BF)

    def ret_low(g, d):
        return rcopy(ret_s.at[0, g, d - 1], ret_r.at[0, g, d - 1], ret_ss.at[0, g, d - 1], ret_rs.at[0, g, d - 1],
                     lax.rem(c + N_CTX - d, N_CTX))

    def ret_up(g, d):
        return rcopy(ret_s.at[1, g, d - 1], ret_r.at[1, g, d - 1], ret_ss.at[1, g, d - 1], ret_rs.at[1, g, d - 1],
                     c + d)

    def ret_fold(g, d):
        return rcopy(ret_s.at[1, g, d - 1], refl_r.at[g, d - 1], ret_ss.at[1, g, d - 1], refl_rs.at[g, d - 1],
                     fold(d))

    def send_low(g):
        for d in range(1, WINDOW + 1):
            ret_low(g, d).start()

    def send_up(g):
        for d in range(1, WINDOW + 1):
            @pl.when(c + d < N_CTX)
            def _():
                ret_up(g, d).start()

            @pl.when((c + d >= N_CTX) & jnp.logical_not(is_self(d)))
            def _():
                ret_fold(g, d).start()
            if d % 2 == 1:
                @pl.when(is_self(d))
                def _():
                    refl_r[g, d - 1] = ret_s[1, g, d - 1]

    def done_ret(g):
        for d in range(1, WINDOW + 1):
            ret_low(g, d).wait_send()
            @pl.when(jnp.logical_not(is_self(d)))
            def _():
                ret_up(g, d).wait_send()

    def wait_ret(g):
        for d in range(1, WINDOW + 1):
            ret_low(g, d).wait_recv()

            @pl.when(c >= d)
            def _():
                ret_up(g, d).wait_recv()

            @pl.when((c >= N_CTX - d) & jnp.logical_not(is_self(d)))
            def _():
                ret_fold(g, d).wait_recv()

    def send_shared(g):
        def send(k):
            j = lax.rem(gi + k, 16)
            zj, rj = j // 2, lax.rem(j, 2)
            dev = at(zj, x, rj)
            rcopy(ps.at[g, rj, :, pl.ds(pl.multiple_of(zj * PIECE, PIECE), PIECE), :], st1.at[g, gi],
                  st1_ss.at[g], st1_rs.at[g], dev).start()
            rcopy(bsrc.at[g], b1.at[g, gi], b1_ss.at[g], b1_rs.at[g], dev).start()
        loop(1, 16, send)

    def step1(g):
        st1[g, gi] = ps[g, core, :, pl.ds(pl.multiple_of(z * PIECE, PIECE), PIECE), :]
        b1[g, gi] = bsrc[g]
        wait_bytes(b1.at[g, pl.ds(0, 15)], b1_rs.at[g])
        total = b1[g, 0]
        for k in range(1, 16):
            total = total + b1[g, k]
        b2s[g] = total
        b2[g, x] = total

        def send(k):
            rcopy(b2s.at[g], b2.at[g, x], b2_ss.at[g], b2_rs.at[g], at(z, lax.rem(x + k, NX), core)).start()
        loop(1, NX, send)
        wait_bytes(st1.at[g, pl.ds(0, 15)], st1_rs.at[g])
        total = st1[g, 0].astype(F32)
        for k in range(1, 16):
            total = total + st1[g, k].astype(F32)
        st2s[g] = total.astype(BF)

        @pl.when(is_root)
        def _():
            st2[g, 0] = st2s[g]

        @pl.when(jnp.logical_not(is_root))
        def _():
            rcopy(st2s.at[g], st2.at[g, z * NX + x], st2_ss.at[g], st2_rs.at[g], core).start()

    def step2(g):
        wait_bytes(b2.at[g, pl.ds(0, NX - 1)], b2_rs.at[g])
        total = b2[g, 0]
        for k in range(1, NX):
            total = total + b2[g, k]
        b3s[g] = total
        b3[g, y] = total

        def send(k):
            ycopy(b3s.at[g], b3.at[g, y], b3_ss.at[g], b3_rs.at[g], lax.rem(y + k, NY)).start()
        loop(1, NY, send)

    def step3(g):
        wait_bytes(b3.at[g, pl.ds(0, NY - 1)], b3_rs.at[g])
        total = b3[g, 0]
        for k in range(1, NY):
            total = total + b3[g, k]
        db_ref[pl.ds(pl.multiple_of(g * 8, 8), 8), :] = total * (1.0 / math.sqrt(ROWS))

    def finish(g):
        wait_ret(g)
        cols = pl.ds(pl.multiple_of(g * 128, 128), 128)
        for kv, out in ((0, dk_ref), (1, dv_ref)):
            first, second = own[0, g, kv], own[1, g, kv]
            for d in range(WINDOW):
                first = first + ret_r[0, g, d, kv].astype(F32) + refl_r[g, d, kv].astype(F32)
                second = second + ret_r[1, g, d, kv].astype(F32)
            own[0, g, kv] = first
            out[0:BLOCK, cols] = first.astype(BF)
            out[BLOCK:2 * BLOCK, cols] = second.astype(BF)

    def finish_root(g):
        wait_bytes(st2.at[g, pl.ds(0, NZ * NX - 1)], st2_rs.at[g])
        cols = pl.ds(pl.multiple_of(g * 128, 128), 128)
        for kv, out in ((0, dk_ref), (1, dv_ref)):
            for p in range(NZ):
                rr = slice(p * PIECE, (p + 1) * PIECE)
                total = own[0, g, kv, rr, :]
                for k in range(NX):
                    total = total + st2[g, p * NX + k, kv].astype(F32)
                out[rr, cols] = total.astype(BF)

    def main(g):
        q_load(q_hbm, qv, q_sem, g).wait()
        q_load(go_hbm, gv, g_sem, g).wait()
        wait_bytes(seven(g), s3_rs.at[g])
        wait_window(g, 0)
        unit(g, 0)
        send_low(g)

        @pl.when(g + 2 < GROUPS)
        def _():
            prompt_row(g + 2)

        @pl.when(g + 1 < GROUPS)
        def _():
            prompt_column(g + 1)

        @pl.when(g > 0)
        def _():
            step1(g - 1)
        wait_window(g, 1)
        unit(g, 1)
        send_shared(g)
        send_up(g)

        @pl.when(g > 0)
        def _():
            step2(g - 1)
    loop(0, GROUPS, main)

    last = GROUPS - 1
    loop(0, last, finish)
    step1(last)
    finish(last)
    step2(last)

    @pl.when(is_root)
    def _():
        loop(0, GROUPS, finish_root)
    loop(0, GROUPS, step3)

    def drain(g):
        done_window(g)
        done_ret(g)

        @pl.when(is_root)
        def _():
            wait_bytes(prompt.at[g, 0, :, pl.ds(0, (NZ - 1) * PIECE), :], s1_ss.at[g])

        @pl.when(jnp.logical_not(is_root))
        def _():
            wait_bytes(st2s.at[g], st2_ss.at[g])

        @pl.when(x == 0)
        def _():
            wait_bytes(prompt.at[g, 0, :, pl.ds(0, 7 * PIECE), :], s2_ss.at[g])
        wait_bytes(seven(g), s3_ss.at[g])
        wait_bytes(st1.at[g, pl.ds(0, 15)], st1_ss.at[g])
        wait_bytes(b1.at[g, pl.ds(0, 15)], b1_ss.at[g])
        wait_bytes(b2.at[g, pl.ds(0, NX - 1)], b2_ss.at[g])
        wait_bytes(b3.at[g, pl.ds(0, NY - 1)], b3_ss.at[g])
    loop(0, GROUPS, drain)


def body(query_in, key_in, value_rows_input, grad_out, query_bias, key_blocks, trace_len):
    any_ = pl.BlockSpec(memory_space=pl.ANY)
    vmem = pl.BlockSpec(memory_space=pltpu.VMEM)
    smem = pl.BlockSpec(memory_space=pltpu.SMEM)
    dma = pltpu.SemaphoreType.DMA
    tile = (2, BLOCK, 128)
    G = GROUPS
    dq, dk, dv, db = pl.pallas_call(
        kernel,
        out_shape=(
            jax.ShapeDtypeStruct((2 * BLOCK, 4096), BF),
            jax.ShapeDtypeStruct((2 * BLOCK, 512), BF),
            jax.ShapeDtypeStruct((2 * BLOCK, 512), BF),
            jax.ShapeDtypeStruct((32, 128), F32),
        ),
        in_specs=[any_, any_, any_, any_, vmem, smem, smem],
        out_specs=(vmem, vmem, vmem, vmem),
        scratch_shapes=[
            pltpu.VMEM((G, 2 * BLOCK, 1024), BF),
            pltpu.VMEM((G, 2 * BLOCK, 1024), BF),
            pltpu.VMEM((2, G) + tile, BF),
            pltpu.VMEM((G, PROMPT) + tile, BF),
            pltpu.VMEM((2, G, WINDOW) + tile, BF),
            pltpu.VMEM((2, G, WINDOW) + tile, BF),
            pltpu.VMEM((2, G, WINDOW) + tile, BF),
            pltpu.VMEM((G, WINDOW) + tile, BF),
            pltpu.VMEM((2, G) + tile, F32),
            pltpu.VMEM((PROMPT,) + tile, F32),
            pltpu.VMEM((G, PROMPT) + tile, BF),
            pltpu.VMEM((G, 16, 2, PIECE, 128), BF),
            pltpu.VMEM((G, 2, PIECE, 128), BF),
            pltpu.VMEM((G, NZ * NX, 2, PIECE, 128), BF),
            pltpu.VMEM((G, 8, 128), F32),
            pltpu.VMEM((G, 16, 8, 128), F32),
            pltpu.VMEM((G, 8, 128), F32),
            pltpu.VMEM((G, NX, 8, 128), F32),
            pltpu.VMEM((G, 8, 128), F32),
            pltpu.VMEM((G, NY, 8, 128), F32),
            dma((G,)), dma((G,)), dma((2, 2, G)),
            dma((3, G, WINDOW)), dma((2, G, WINDOW)),
            dma((G,)), dma((G,)), dma((G,)), dma((G, PROMPT)), dma((G,)), dma((G,)),
            dma((2, G, WINDOW)), dma((2, G, WINDOW)), dma((G, WINDOW)),
            dma((G,)), dma((G,)), dma((G,)), dma((G,)),
            dma((G,)), dma((G,)), dma((G,)), dma((G,)), dma((G,)), dma((G,)),
        ],
        compiler_params=pltpu.CompilerParams(
            collective_id=0, has_side_effects=True, vmem_limit_bytes=58 * 2**20),
        name="attention",
    )(query_in[0], key_in[0], value_rows_input[0], grad_out[0], query_bias.reshape(32, 128), key_blocks, trace_len)
    return dq[None], dk[None], dv[None], db.reshape(4096)


def solution(mesh):
    return jax.shard_map(
        body,
        mesh=mesh,
        in_specs=(
            P("dp", "ctx", None),
            P("dp", "ctx", None),
            P("dp", "ctx", None),
            P("dp", "ctx", None),
            P(),
            P("dp", None, None),
            P("dp"),
        ),
        out_specs=(P("dp", "ctx", None), P("dp", "ctx", None), P("dp", "ctx", None), P()),
        check_vma=False,
    )
```

time: 595 us -> 102 us (0.17)
  waiting for transfers between devices: 247 us -> 0 us
  blocking collectives: 93.1 us -> 0 us
  Pallas kernels: 0 us -> 92.5 us
  matrix products: 71.3 us -> 0 us
  local copies, waits for them, and re-layouts: 70.5 us -> 6.63 us
  starting transfers between devices: 55.6 us -> 0 us
  other arithmetic: 34.3 us -> 0 us
  between operations: 15.7 us -> 1.31 us
    psum x2 -> x0, waiting for transfers between devices: 235 us -> none  [the longest x1 161 us: broadcast(): return lax.psum(kept, axis)]
    psum x1 -> x0, blocking collectives: 93.1 us -> none  [body(): bias_total = lax.psum(local_bias, ('ctx', 'dp'))]
    pallas_call x0 -> x1, Pallas kernels: none -> 92.5 us  [body(): pl.pallas_call(kernel, out_shape=(jax.ShapeDtypeStruct((2 * BLOCK, 4096),...]
    dot_general x15 -> x0, matrix products: 71.3 us -> none  [the longest x2 17.5 us: body(): jnp.einsum('dn,tdbf->tnbf', chooser[half_idx].astype(jnp.float32), contri...]
    ppermute x12 -> x0, starting transfers between devices: 55.5 us -> none  [from_behind(): lax.ppermute(value, axis, [(source, source + steps) for source in range(i...]
    slice x12 -> x0, local copies, waits for them, and re-layouts: 20.9 us -> none  [the longest x4 5.24 us: body(): candidates[..., :width_kv]]
    another operation x9 -> x0, local copies, waits for them, and re-layouts: 13 us -> none
    ppermute x12 -> x0, waiting for transfers between devices: 11.9 us -> none  [from_behind(): lax.ppermute(value, axis, [(source, source + steps) for source in range(i...]
  transfers between devices with their start and end apart: 14 -> 0, of which waited for: 4 -> 0; matrix products, arithmetic and copies ran while one was open for 9% -> 0% of each run, Pallas kernels for 0% -> 0%
where the time goes in v1:
time: 102 us; the launch traced here: 100 us
  Pallas kernels  92.5 us (91%)
  local copies, waits for them, and re-layouts  6.63 us (6%)
  between operations  1.31 us (1%)
    pallas_call x1, Pallas kernels, body(): pl.pallas_call(kernel, out_shape=(jax.ShapeDtypeStruct((2 * BLOCK, 4096),...  92.5 us
    unnamed x11, local copies, waits for them, and re-layouts  6.63 us

profile of v1, /device:TPU:1, one launch (start us, length us, event | category | flops | bytes accessed | tf_op | source)
XLA Modules:
  0.0 100.4 jit_solution(9373526017041361976)
XLA Ops:
  1.3 1.4 %copy.11.kb_ref = s32[1,128,6]{2,1,0:T(8,128)} copy(s32[1,128,6]{1,0,2:T(1,128)} %param.12) | data formatting | bytes 6144 | tf_op args[5]
  2.7 92.5 %attention.1 = (bf16[256,4096]{1,0:T(8,128)(2,1)}, bf16[256,512]{1,0:T(8,128)(2,1)}, bf16[256,512]{1,0:T(8,128)(2,1)}, f32[32,128]{1,0:T(8,128)}) custom-call(bf16[256,4096]{1,0:T(8,128)(2,1)} %bitcast.9, bf16[256,512]{1,0:T(8,128)(2,1)} %bitcast.12, bf16[256,512]{1,0:T(8,128)(2,1)} %bitcast.13, bf16[256,4096]{1,0:T(8,128)(2,1)} %bitcast.10, ...), custom_call_target="tpu_custom_call" | custom-call | tf_op jit(solution)/shard_map/attention/pallas_call | solution.py:496
  95.2 0.0 copy-start.1
  95.2 0.0 copy-start
  95.2 0.0 copy-start.2
  95.2 3.2 %copy.17 = bf16[1,256,4096]{2,1,0:T(8,128)(2,1)} copy(bf16[1,256,4096]{2,1,0:T(8,128)(2,1)} %bitcast.11) | data formatting | bytes 4194304
  98.4 0.0 copy-done.1
  98.4 0.7 copy.18
  99.1 0.0 copy-done
  99.1 0.7 copy.19
  99.8 0.0 copy-done.2
  99.8 0.6 copy.20
Async XLA Ops:
  95.2 3.2 %copy-start.1 = (bf16[256,512]{1,0:T(8,128)(2,1)S(1)}, bf16[256,512]{1,0:T(8,128)(2,1)}, u32[]{:S(2)}) copy-start(bf16[256,512]{1,0:T(8,128)(2,1)} %get-tuple-element.9) | copy-start | bytes 786436
  95.2 3.9 %copy-start = (bf16[256,512]{1,0:T(8,128)(2,1)S(1)}, bf16[256,512]{1,0:T(8,128)(2,1)}, u32[]{:S(2)}) copy-start(bf16[256,512]{1,0:T(8,128)(2,1)} %get-tuple-element.10) | copy-start | bytes 786436
  95.2 4.6 %copy-start.2 = (f32[32,128]{1,0:T(8,128)S(1)}, f32[32,128]{1,0:T(8,128)}, u32[]{:S(2)}) copy-start(f32[32,128]{1,0:T(8,128)} %get-tuple-element.11) | copy-start | bytes 49156

commit v2 on v1

v2 whole, which is shorter than its diff:
```python
import math

import jax
import jax.numpy as jnp
from jax import lax
from jax.experimental import pallas as pl
from jax.experimental.pallas import tpu as pltpu
from jax.sharding import PartitionSpec as P

HEAD_SIZE = 128
BLOCK = 128
PROMPT = 2
WINDOW = 3
NBLK = 128
N_CTX = 64
CHIPS = 32
NZ, NX, NY = 8, 4, 4
GROUPS = 2
PER_GROUP = 8
PIECE = BLOCK // NZ
SLOTS = PROMPT + WINDOW + 1
NEAR = 5
ROWS = 65536
SCALE = HEAD_SIZE ** (-0.5)
SCALE2 = SCALE * math.log2(math.e)
FAR = -1e30
BF, F32 = jnp.bfloat16, jnp.float32
MESH = pl.DeviceIdType.MESH


def dot(a, b, ca, cb):
    return lax.dot_general(a, b, (((ca,), (cb,)), ((), ())), preferred_element_type=F32)


def kernel(q_hbm, k_hbm, v_hbm, go_hbm, bias_ref, kb_ref, tl_ref,
           dq_ref, dk_ref, dv_ref, db_ref,
           qv, gv, stage, prompt, cand, acc, pacc, dqs, ret_s, ret_r, refl_r, sib_s, sib_r,
           ps, st1, st2s, st2, st3s, st3, bsrc, b1, b2s, b2, b3s, b3,
           q_sem, g_sem, kv_sem, own_sem, qx_ss, qx_rs, gx_ss, gx_rs, cx_ss, cx_rs,
           win_ss, win_rs, s1_ss, s1_rs, s2_ss, s2_rs, s3_ss, s3_rs, dq_ss, dq_rs,
           ret_ss, ret_rs, refl_rs, sib_ss, sib_rs, st1_ss, st1_rs, st2_ss, st2_rs, st3_ss, st3_rs,
           b1_ss, b1_rs, b2_ss, b2_rs, b3_ss, b3_rs):
    c = lax.axis_index("ctx")
    y = lax.axis_index("dp")
    core = lax.rem(c, 2)
    other = 1 - core
    chip = c // 2
    x = lax.rem(chip, NX)
    z = chip // NX
    sibling = chip * 2 + other
    is_root = c < PROMPT

    def at(zz, xx, rr):
        return (zz * NX + xx) * 2 + rr

    def rcopy(src, dst, ss, rs, dev):
        return pltpu.make_async_remote_copy(src_ref=src, dst_ref=dst, send_sem=ss, recv_sem=rs,
                                            device_id={"ctx": dev}, device_id_type=MESH)

    def wait_bytes(ref, sem):
        pltpu.make_async_copy(ref, ref, sem).wait()

    def loop(lo, hi, f):
        def step(i, carry):
            f(i)
            return carry
        lax.fori_loop(lo, hi, step, 0)

    def span(start, size):
        return pl.ds(pl.multiple_of(start, size), size)

    def kv_copy(half, kv, head, dst, sem):
        src = k_hbm if kv == 0 else v_hbm
        return pltpu.make_async_copy(src.at[half * BLOCK:(half + 1) * BLOCK, span(head * 128, 128)], dst, sem)

    def mine(half):
        return other if half == 0 else core

    def kv_stage(half, kv, head):
        return kv_copy(half, kv, head, stage.at[half, head, kv], kv_sem.at[half, kv, head])

    def kv_own(half, kv, g):
        return kv_copy(half, kv, core * 2 + g, cand.at[half, g, mine(half), kv], own_sem.at[half, kv, g])

    def q_own(src, dst, sem, g):
        return pltpu.make_async_copy(src.at[:, span(core * 2048 + g * 1024, 1024)], dst.at[1, g], sem.at[g])

    def q_cross(src, dst, ss, rs, g):
        return rcopy(src.at[:, span(other * 2048 + g * 1024, 1024)], dst.at[0, g], ss.at[g], rs.at[g], sibling)

    def start_stage(h):
        for half in range(2):
            for kv in range(2):
                kv_stage(half, kv, h).start()
    loop(0, 4, start_stage)

    def start_own(g):
        for half in range(2):
            for kv in range(2):
                kv_own(half, kv, g).start()
        q_own(q_hbm, qv, q_sem, g).start()
        q_own(go_hbm, gv, g_sem, g).start()
    loop(0, GROUPS, start_own)

    barrier = pltpu.get_barrier_semaphore()

    def greet(dev, yy):
        pl.semaphore_signal(barrier, inc=1, device_id={"ctx": dev, "dp": yy}, device_id_type=MESH)

    def greet_near(k):
        away = lax.rem(chip + CHIPS - 2 + k, CHIPS)

        @pl.when(k != 2)
        def _():
            greet(away * 2, y)
            greet(away * 2 + 1, y)
    loop(0, 5, greet_near)

    gi = z * 2 + core

    def greet_group(k):
        j = lax.rem(gi + k, 16)
        greet(at(j // 2, x, lax.rem(j, 2)), y)
    loop(1, 16, greet_group)

    def greet_row(k):
        greet(at(z, lax.rem(x + k, NX), core), y)
    loop(1, NX, greet_row)

    def greet_y(k):
        yy = lax.rem(y + k, NY)
        greet(c, yy)
        greet(sibling, yy)
    loop(1, NY, greet_y)

    def zero(g):
        for half in range(2):
            ret_r[half, g] = jnp.zeros((2, 2, 2, BLOCK, 128), BF)
            acc[half, g] = jnp.zeros((NEAR, 2, BLOCK, 128), F32)
        refl_r[g] = jnp.zeros((2, 2, BLOCK, 128), BF)
        pacc[g] = jnp.zeros((PROMPT, 2, BLOCK, 128), F32)
        bsrc[g] = jnp.zeros((8, 128), F32)
    loop(0, GROUPS, zero)

    def wait_stage(h):
        for half in range(2):
            for kv in range(2):
                kv_stage(half, kv, h).wait()
    loop(0, 4, wait_stage)

    pl.semaphore_wait(barrier, 8 + 15 + 3 + 6)

    def rows16(p):
        return span(p * PIECE, PIECE)

    @pl.when(is_root)
    def _():
        def scatter_group(g):
            prompt[g, c, :, 0:PIECE, :] = stage[0, c * 2 + g, :, 0:PIECE, :]

            def scatter(k):
                j = lax.rem(c + k, 16)
                p, r = j // 2, lax.rem(j, 2)
                rcopy(stage.at[0, r * 2 + g, :, rows16(p), :], prompt.at[g, c, :, rows16(p), :],
                      s1_ss.at[g], s1_rs.at[g, c], at(p, 0, r)).start()
            loop(1, 16, scatter)
        loop(0, GROUPS, scatter_group)

    def win_low(g, r, far):
        dst = lax.rem(chip + 1 + far, CHIPS) * 2 + r
        slot = 4 if far else 1 + 2 - core
        return rcopy(stage.at[0, r * 2 + g], cand.at[0, g, slot], win_ss.at[0, g, r, far], win_rs.at[0, g, slot - 2], dst)

    def win_up(g, r, far):
        dst = (chip - 1 - far) * 2 + r
        slot = 4 if far else 1 + 1 + core
        return rcopy(stage.at[1, r * 2 + g], cand.at[1, g, slot], win_ss.at[1, g, r, far], win_rs.at[1, g, slot - 2], dst)

    def win_fold(g, r):
        return rcopy(stage.at[0, r * 2 + g], cand.at[1, g, 4], win_ss.at[1, g, r, 1], win_rs.at[1, g, 2],
                     N_CTX - 4 + r)

    def cross(half, g):
        slot = mine(half)
        return rcopy(stage.at[half, other * 2 + g], cand.at[half, g, slot], cx_ss.at[half, g], cx_rs.at[half, g], sibling)

    def each_window(g, act):
        for r in range(2):
            act(win_low(g, r, 0))

            @pl.when(chip >= 1)
            def _():
                act(win_up(g, r, 0))

            @pl.when(core == 1)
            def _():
                act(win_low(g, r, 1))

            @pl.when((core == 0) & (chip >= 2))
            def _():
                act(win_up(g, r, 1))

            @pl.when(c == N_CTX - 1)
            def _():
                act(win_fold(g, r))
        for half in range(2):
            act(cross(half, g))
        act(q_cross(q_hbm, qv, qx_ss, qx_rs, g))
        act(q_cross(go_hbm, gv, gx_ss, gx_rs, g))

    def wait_near(g, half):
        cross(half, g).wait_recv()
        for slot in range(2, NEAR):
            rcopy(cand.at[half, g, slot], cand.at[half, g, slot], win_ss.at[0, g, 0, 0], win_rs.at[half, g, slot - 2],
                  sibling).wait_recv()

    def prompt_piece(g):
        return prompt.at[g, :, :, rows16(z), :]

    def prompt_row(g):
        @pl.when(x == 0)
        def _():
            for r in range(PROMPT):
                @pl.when(c != r)
                def _():
                    wait_bytes(prompt.at[g, r, :, rows16(z), :], s1_rs.at[g, r])

            def send(k):
                rcopy(prompt_piece(g), prompt_piece(g), s2_ss.at[g], s2_rs.at[g], at(z, k, core)).start()
            loop(1, NX, send)

    def prompt_column(g):
        @pl.when(x > 0)
        def _():
            wait_bytes(prompt_piece(g), s2_rs.at[g])

        def send(k):
            rcopy(prompt_piece(g), prompt_piece(g), s3_ss.at[g], s3_rs.at[g], at(lax.rem(z + k, NZ), x, core)).start()
        loop(1, NZ, send)

    def pieces(ref, g, n):
        return ref.at[g, :, :, pl.ds(0, n * PIECE), :]

    each_window(0, lambda copy: copy.start())
    prompt_row(0)
    prompt_column(0)
    each_window(1, lambda copy: copy.start())
    prompt_row(1)

    width = PER_GROUP * 128
    kk = lax.broadcasted_iota(jnp.int32, (BLOCK, width), 0)
    qi = lax.rem(lax.broadcasted_iota(jnp.int32, (BLOCK, width), 1), BLOCK)
    lane = lax.rem(lax.broadcasted_iota(jnp.int32, (1, width), 1), BLOCK)
    length = tl_ref[0]

    def unit(g, half, role):
        rho = core if role else other
        dev = chip * 2 + rho
        blk = jnp.where(half == 0, dev, NBLK - 1 - dev)
        base = jnp.where(half == 0, 1 - rho, rho)
        rows = span(half * BLOCK, BLOCK)
        bias = bias_ref[span(core * 16 + g * 8, 8), :]
        Q = jnp.concatenate(
            [(qv[role, g, rows, j * 128:(j + 1) * 128].astype(F32) + bias[j:j + 1]).astype(BF)
             for j in range(PER_GROUP)], 0)
        G = jnp.concatenate([gv[role, g, rows, j * 128:(j + 1) * 128] for j in range(PER_GROUP)], 0)
        K, V = (jnp.concatenate(
            [prompt[g, s, kv] for s in range(PROMPT)] + [cand[half, g, base + d, kv] for d in range(WINDOW + 1)], 0)
            for kv in range(2))
        off = [jnp.where(kb_ref[s * NBLK + blk] >= 0, 0.0, FAR).astype(F32) for s in range(SLOTS)]
        S = dot(K, Q, 1, 1)
        parts, m = [], None
        for s in range(SLOTS):
            v = S[s * 128:(s + 1) * 128]
            if s == PROMPT:
                v = jnp.where(kk <= qi, v, FAR)
            parts.append(v)
            mm = jnp.max(v, 0, keepdims=True) + off[s]
            m = mm if m is None else jnp.maximum(m, mm)
        m = m * SCALE2
        exps, tot = [], None
        for s in range(SLOTS):
            p = jnp.exp2(parts[s] * SCALE2 - (m - off[s]))
            exps.append(p)
            t = jnp.sum(p, 0, keepdims=True)
            tot = t if tot is None else tot + t
        inv = jnp.where(blk * BLOCK + lane < length, 1.0 / tot, 0.0)
        probs = jnp.concatenate(exps, 0) * inv
        low = probs.astype(BF)
        dP = dot(V, G, 1, 1)
        r = jnp.sum(low.astype(F32) * dP, 0, keepdims=True)
        dS = (probs * (dP - r)).astype(BF)
        dv = dot(low, G, 1, 0)
        dk = dot(dS, Q, 1, 0) * SCALE
        dqT = dot(K, dS, 0, 0)
        for j in range(PER_GROUP):
            t = dqT[:, j * 128:(j + 1) * 128].T * SCALE
            if role:
                dq_ref[rows, span(core * 2048 + g * 1024 + j * 128, 128)] = t.astype(BF)
            else:
                dqs[g, rows, j * 128:(j + 1) * 128] = t.astype(BF)
            bsrc[g, j:j + 1, :] = bsrc[g, j:j + 1, :] + jnp.sum(t, 0, keepdims=True)
        for kv, val in ((0, dk), (1, dv)):
            for s in range(PROMPT):
                pacc[g, s, kv] = pacc[g, s, kv] + val[s * 128:(s + 1) * 128]
            for d in range(WINDOW + 1):
                acc[half, g, base + d, kv] = acc[half, g, base + d, kv] + val[256 + d * 128:384 + d * 128]

    def dq_cross(g, half):
        rows = span(half * BLOCK, BLOCK)
        return rcopy(dqs.at[g, rows, :], dq_ref.at[rows, span(core * 2048 + g * 1024, 1024)],
                     dq_ss.at[g, half], dq_rs.at[g, half], sibling)

    def ret_low(g, e):
        far = 1 if e == 3 else 0
        return rcopy(ret_s.at[0, g, e - 1], ret_r.at[0, g, core, far], ret_ss.at[0, g, e - 1],
                     ret_rs.at[0, g, core, far], lax.rem(chip * 2 + N_CTX - e, N_CTX))

    def ret_up(g, e):
        far = 1 if e == 3 else 0
        return rcopy(ret_s.at[1, g, e - 1], ret_r.at[1, g, core, far], ret_ss.at[1, g, e - 1],
                     ret_rs.at[1, g, core, far], chip * 2 + 1 + e)

    def ret_fold(g):
        return rcopy(ret_s.at[1, g, 2], refl_r.at[g, core], ret_ss.at[1, g, 2], refl_rs.at[g, core], N_CTX - 1)

    def sib_copy(g, half):
        return rcopy(sib_s.at[half, g], sib_r.at[half, g], sib_ss.at[half, g], sib_rs.at[half, g], sibling)

    def each_low(g, act):
        for e in range(1, WINDOW + 1):
            act(ret_low(g, e))
        act(sib_copy(g, 0))

    def each_up(g, act):
        for e in range(1, WINDOW + 1):
            @pl.when(chip * 2 + 1 + e < N_CTX)
            def _():
                act(ret_up(g, e))

        @pl.when(chip == CHIPS - 2)
        def _():
            act(ret_fold(g))
        act(sib_copy(g, 1))

    def send_low(g):
        for e in range(WINDOW):
            ret_s[0, g, e] = acc[0, g, 2 + e].astype(BF)
        sib_s[0, g] = acc[0, g, core].astype(BF)
        each_low(g, lambda copy: copy.start())

    def send_up(g):
        for e in range(WINDOW):
            ret_s[1, g, e] = acc[1, g, 2 + e].astype(BF)
        sib_s[1, g] = acc[1, g, other].astype(BF)
        each_up(g, lambda copy: copy.start())

    def fold_sums(g):
        for e in range(WINDOW):
            acc[0, g, e] = acc[0, g, e] + acc[1, g, 2 + e]

    def wait_recv(ref, sem):
        rcopy(ref, ref, win_ss.at[0, 0, 0, 0], sem, sibling).wait_recv()

    def wait_ret(g):
        for r in range(2):
            wait_recv(ret_r.at[0, g, r, 0], ret_rs.at[0, g, r, 0])

            @pl.when(core == 1)
            def _():
                wait_recv(ret_r.at[0, g, r, 1], ret_rs.at[0, g, r, 1])

            @pl.when(chip >= 1)
            def _():
                wait_recv(ret_r.at[1, g, r, 0], ret_rs.at[1, g, r, 0])

            @pl.when((core == 0) & (chip >= 2))
            def _():
                wait_recv(ret_r.at[1, g, r, 1], ret_rs.at[1, g, r, 1])

            @pl.when(c == N_CTX - 1)
            def _():
                wait_recv(refl_r.at[g, r], refl_rs.at[g, r])
        for half in range(2):
            wait_recv(sib_r.at[half, g], sib_rs.at[half, g])

    def send_shared(g):
        ps[g] = pacc[g].astype(BF)

        def send(k):
            zj = lax.rem(z + k, NZ)
            dev = at(zj, x, core)
            rcopy(ps.at[g, :, :, rows16(zj), :], st1.at[g, z], st1_ss.at[g], st1_rs.at[g], dev).start()
            rcopy(bsrc.at[g], b1.at[g, z], b1_ss.at[g], b1_rs.at[g], dev).start()
        loop(1, NZ, send)
        st1[g, z] = ps[g, :, :, rows16(z), :]
        b1[g, z] = bsrc[g]

    def total_of(ref, g, n):
        total = ref[g, 0].astype(F32)
        for k in range(1, n):
            total = total + ref[g, k].astype(F32)
        return total

    def step1(g):
        wait_bytes(st1.at[g, pl.ds(0, NZ - 1)], st1_rs.at[g])
        st2s[g] = total_of(st1, g, NZ).astype(BF)

        @pl.when(x == 0)
        def _():
            st2[g, 0] = st2s[g]

        @pl.when(x > 0)
        def _():
            rcopy(st2s.at[g], st2.at[g, x], st2_ss.at[g], st2_rs.at[g], at(z, 0, core)).start()
        wait_bytes(b1.at[g, pl.ds(0, NZ - 1)], b1_rs.at[g])
        total = total_of(b1, g, NZ)
        b2s[g] = total
        b2[g, x] = total

        def send(k):
            rcopy(b2s.at[g], b2.at[g, x], b2_ss.at[g], b2_rs.at[g], at(z, lax.rem(x + k, NX), core)).start()
        loop(1, NX, send)

    def to_root(g, root):
        return rcopy(st3s.at[g, root], st3.at[g, core * NZ + z], st3_ss.at[g, root], st3_rs.at[g], root)

    def step2(g):
        @pl.when(x == 0)
        def _():
            wait_bytes(st2.at[g, pl.ds(0, NX - 1)], st2_rs.at[g])
            st3s[g] = total_of(st2, g, NX).astype(BF)
            for root in range(PROMPT):
                @pl.when(c == root)
                def _():
                    st3[g, root * NZ] = st3s[g, root]

                @pl.when(c != root)
                def _():
                    to_root(g, root).start()
        wait_bytes(b2.at[g, pl.ds(0, NX - 1)], b2_rs.at[g])
        total = total_of(b2, g, NX)
        b3s[g] = total
        b3[g, core * NY + y] = total

        def send(k):
            j = lax.rem(core * NY + y + k, 2 * NY)
            pltpu.make_async_remote_copy(
                src_ref=b3s.at[g], dst_ref=b3.at[g, core * NY + y], send_sem=b3_ss.at[g], recv_sem=b3_rs.at[g],
                device_id={"ctx": chip * 2 + j // NY, "dp": lax.rem(j, NY)}, device_id_type=MESH).start()
        loop(1, 2 * NY, send)

    def step3(g):
        wait_bytes(b3.at[g, pl.ds(0, 2 * NY - 1)], b3_rs.at[g])
        for r in range(2):
            total = b3[g, r * NY]
            for k in range(1, NY):
                total = total + b3[g, r * NY + k]
            db_ref[span(r * 16 + g * 8, 8), :] = total * (1.0 / math.sqrt(ROWS))

    def finish(g):
        wait_ret(g)
        for t in range(2):
            r = other if t else core
            cols = span((r * 2 + g) * 128, 128)
            for half in range(2):
                for kv, out in ((0, dk_ref), (1, dv_ref)):
                    total = sib_r[half, g, kv].astype(F32) if t else acc[half, g, mine(half), kv]
                    for far in range(2):
                        total = total + ret_r[half, g, r, far, kv].astype(F32)
                    if half == 0:
                        total = total + refl_r[g, r, kv].astype(F32)

                        @pl.when(is_root)
                        def _():
                            pacc[g, t, kv] = total
                    out[half * BLOCK:(half + 1) * BLOCK, cols] = total.astype(BF)

    def finish_root(g):
        wait_bytes(st3.at[g, pl.ds(0, 2 * NZ - 1)], st3_rs.at[g])
        for t in range(2):
            r = other if t else core
            cols = span((r * 2 + g) * 128, 128)
            for kv, out in ((0, dk_ref), (1, dv_ref)):
                for p in range(NZ):
                    rr = slice(p * PIECE, (p + 1) * PIECE)
                    out[rr, cols] = (pacc[g, t, kv, rr, :] + st3[g, r * NZ + p, kv].astype(F32)).astype(BF)

    def main(i):
        g, half = i // 2, lax.rem(i, 2)

        @pl.when(half == 0)
        def _():
            for kv in range(2):
                kv_own(0, kv, g).wait()
                kv_own(1, kv, g).wait()
            q_own(q_hbm, qv, q_sem, g).wait()
            q_own(go_hbm, gv, g_sem, g).wait()
            q_cross(q_hbm, qv, qx_ss, qx_rs, g).wait_recv()
            q_cross(go_hbm, gv, gx_ss, gx_rs, g).wait_recv()
            wait_near(g, 0)
            wait_bytes(pieces(prompt, g, NZ - 1), s3_rs.at[g])

        @pl.when(half == 1)
        def _():
            cross(1, g).wait_recv()

            @pl.when(chip < CHIPS - 1)
            def _():
                for slot in range(2, NEAR):
                    wait_recv(cand.at[1, g, slot], win_rs.at[1, g, slot - 2])

            @pl.when(chip == CHIPS - 1)
            def _():
                for slot in range(2, NEAR):
                    cand[1, g, slot] = cand[0, g, slot - 2]
        unit(g, half, 0)
        dq_cross(g, half).start()

        @pl.when(i == 0)
        def _():
            prompt_column(1)

        @pl.when(i == 2)
        def _():
            step1(0)
        unit(g, half, 1)

        @pl.when(half == 1)
        def _():
            send_shared(g)

            @pl.when(chip == CHIPS - 1)
            def _():
                fold_sums(g)
                send_low(g)
            send_up(g)

        @pl.when((half == 0) & (chip < CHIPS - 1))
        def _():
            send_low(g)

        @pl.when(i == 2)
        def _():
            step2(0)
    loop(0, 2 * GROUPS, main)

    finish(0)
    step1(1)
    finish(1)
    step2(1)
    step3(0)

    @pl.when(is_root)
    def _():
        loop(0, GROUPS, finish_root)
    step3(1)

    def drain(g):
        for half in range(2):
            dq_cross(g, half).wait()
        each_window(g, lambda copy: copy.wait_send())
        each_low(g, lambda copy: copy.wait_send())
        each_up(g, lambda copy: copy.wait_send())

        @pl.when(is_root)
        def _():
            wait_bytes(st3.at[g, pl.ds(0, 2 * NZ - 1)], s1_ss.at[g])

        @pl.when(x == 0)
        def _():
            wait_bytes(pieces(prompt, g, NX - 1), s2_ss.at[g])
            for root in range(PROMPT):
                @pl.when(c != root)
                def _():
                    to_root(g, root).wait_send()

        @pl.when(x > 0)
        def _():
            wait_bytes(st2s.at[g], st2_ss.at[g])
        wait_bytes(pieces(prompt, g, NZ - 1), s3_ss.at[g])
        wait_bytes(st1.at[g, pl.ds(0, NZ - 1)], st1_ss.at[g])
        wait_bytes(b1.at[g, pl.ds(0, NZ - 1)], b1_ss.at[g])
        wait_bytes(b2.at[g, pl.ds(0, NX - 1)], b2_ss.at[g])
        wait_bytes(b3.at[g, pl.ds(0, 2 * NY - 1)], b3_ss.at[g])
    loop(0, GROUPS, drain)


def body(query_in, key_in, value_rows_input, grad_out, query_bias, key_blocks, trace_len):
    any_ = pl.BlockSpec(memory_space=pl.ANY)
    vmem = pl.BlockSpec(memory_space=pltpu.VMEM)
    smem = pl.BlockSpec(memory_space=pltpu.SMEM)
    dma = pltpu.SemaphoreType.DMA
    tile = (2, BLOCK, 128)
    G = GROUPS

    def many(*dims):
        return pltpu.VMEM(dims + tile, BF)
    part = (PROMPT, 2, PIECE, 128)
    dq, dk, dv, db = pl.pallas_call(
        kernel,
        out_shape=(
            pltpu.VMEM((2 * BLOCK, 4096), BF),
            pltpu.VMEM((2 * BLOCK, 512), BF),
            pltpu.VMEM((2 * BLOCK, 512), BF),
            pltpu.VMEM((32, 128), F32),
        ),
        in_specs=[any_, any_, any_, any_, vmem, smem, smem],
        out_specs=(vmem, vmem, vmem, vmem),
        scratch_shapes=[
            pltpu.VMEM((2, G, 2 * BLOCK, 1024), BF), pltpu.VMEM((2, G, 2 * BLOCK, 1024), BF),
            many(2, 4), many(G, PROMPT), many(2, G, NEAR),
            pltpu.VMEM((2, G, NEAR) + tile, F32), pltpu.VMEM((G, PROMPT) + tile, F32),
            pltpu.VMEM((G, 2 * BLOCK, 1024), BF),
            many(2, G, WINDOW), many(2, G, 2, 2), many(G, 2), many(2, G), many(2, G),
            many(G, PROMPT),
            pltpu.VMEM((G, NZ) + part, BF), pltpu.VMEM((G,) + part, BF), pltpu.VMEM((G, NX) + part, BF),
            pltpu.VMEM((G,) + part, BF), pltpu.VMEM((G, 2 * NZ, 2, PIECE, 128), BF),
            pltpu.VMEM((G, 8, 128), F32), pltpu.VMEM((G, NZ, 8, 128), F32),
            pltpu.VMEM((G, 8, 128), F32), pltpu.VMEM((G, NX, 8, 128), F32),
            pltpu.VMEM((G, 8, 128), F32), pltpu.VMEM((G, 2 * NY, 8, 128), F32),
            dma((G,)), dma((G,)), dma((2, 2, 4)), dma((2, 2, G)),
            dma((G,)), dma((G,)), dma((G,)), dma((G,)), dma((2, G)), dma((2, G)),
            dma((2, G, 2, 2)), dma((2, G, WINDOW)),
            dma((G,)), dma((G, PROMPT)), dma((G,)), dma((G,)), dma((G,)), dma((G,)), dma((G, 2)), dma((G, 2)),
            dma((2, G, WINDOW)), dma((2, G, 2, 2)), dma((G, 2)), dma((2, G)), dma((2, G)),
            dma((G,)), dma((G,)), dma((G,)), dma((G,)), dma((G, PROMPT)), dma((G,)),
            dma((G,)), dma((G,)), dma((G,)), dma((G,)), dma((G,)), dma((G,)),
        ],
        compiler_params=pltpu.CompilerParams(
            collective_id=0, has_side_effects=True, vmem_limit_bytes=58 * 2**20),
        name="attention",
    )(query_in[0], key_in[0], value_rows_input[0], grad_out[0], query_bias.reshape(32, 128),
      key_blocks.transpose(2, 0, 1).reshape(-1), trace_len)
    return dq[None], dk[None], dv[None], db.reshape(4096)


def solution(mesh):
    return jax.shard_map(
        body,
        mesh=mesh,
        in_specs=(
            P("dp", "ctx", None),
            P("dp", "ctx", None),
            P("dp", "ctx", None),
            P("dp", "ctx", None),
            P(),
            P("dp", None, None),
            P("dp"),
        ),
        out_specs=(P("dp", "ctx", None), P("dp", "ctx", None), P("dp", "ctx", None), P()),
        check_vma=False,
    )
```

time: 102 us -> 77.6 us (0.76); the launches traced: 100 us -> 77.4 us
  Pallas kernels: 92.5 us -> 72.2 us
  local copies, waits for them, and re-layouts: 6.63 us -> 3.96 us
    pallas_call x1, Pallas kernels: 92.5 us -> 72.2 us  [body(): pl.pallas_call(kernel, out_shape=(pltpu.VMEM((2 * BLOCK, 4096), BF), pltp...]
    unnamed x11 -> x6, local copies, waits for them, and re-layouts: 6.63 us -> 3.36 us
where the time goes in v2:
time: 77.6 us; the launch traced here: 77.4 us
  Pallas kernels  72.2 us (93%)
  local copies, waits for them, and re-layouts  3.96 us (5%)
  between operations  1.31 us (2%)
    pallas_call x1, Pallas kernels, body(): pl.pallas_call(kernel, out_shape=(pltpu.VMEM((2 * BLOCK, 4096), BF), pltp...  72.2 us
    unnamed x6, local copies, waits for them, and re-layouts  3.36 us

profile of v2, /device:TPU:1, one launch (start us, length us, event | category | flops | bytes accessed | tf_op | source)
XLA Modules:
  0.0 77.4 jit_solution(4951657070072448199)
XLA Ops:
  0.6 0.0 copy-start
  1.3 0.0 copy-done
  1.3 0.6 bitcast_reduce_fusion
  1.9 72.2 %attention.1 = (bf16[256,4096]{1,0:T(8,128)(2,1)S(1)}, bf16[256,512]{1,0:T(8,128)(2,1)S(1)}, bf16[256,512]{1,0:T(8,128)(2,1)S(1)}, f32[32,128]{1,0:T(8,128)S(1)}) custom-call(bf16[256,4096]{1,0:T(8,128)(2,1)} %bitcast.16, bf16[256,512]{1,0:T(8,128)(2,1)} %bitcast.18, bf16[256,512]{1,0:T(8,128)(2,1)} %bitcast.19, bf16[256,4096]{1,0:T(8,128)(2,1)} %bitcast.17, ...), custom_call_target="tpu_custom_call" | custom-call | tf_op jit(solution)/shard_map/attention/pallas_call | solution.py:600
  74.1 1.3 %copy.15 = bf16[1,256,4096]{2,1,0:T(8,128)(2,1)} copy(bf16[1,256,4096]{2,1,0:T(8,128)(2,1)S(1)} %bitcast.12) | data formatting | bytes 4194304
  75.4 0.7 copy.16
  76.1 0.6 copy.18
  76.7 0.7 copy.17
Async XLA Ops:
  0.6 0.7 copy-start

commit v3 on v2

--- a/solution.py
+++ b/solution.py
@@ -153,9 +153,9 @@
     def rows16(p):
         return span(p * PIECE, PIECE)
 
-    @pl.when(is_root)
-    def _():
-        def scatter_group(g):
+    def scatter_prompt(g):
+        @pl.when(is_root)
+        def _():
             prompt[g, c, :, 0:PIECE, :] = stage[0, c * 2 + g, :, 0:PIECE, :]
 
             def scatter(k):
@@ -164,7 +164,7 @@
                 rcopy(stage.at[0, r * 2 + g, :, rows16(p), :], prompt.at[g, c, :, rows16(p), :],
                       s1_ss.at[g], s1_rs.at[g, c], at(p, 0, r)).start()
             loop(1, 16, scatter)
-        loop(0, GROUPS, scatter_group)
+    scatter_prompt(0)
 
     def win_low(g, r, far):
         dst = lax.rem(chip + 1 + far, CHIPS) * 2 + r
@@ -244,8 +244,6 @@
     each_window(0, lambda copy: copy.start())
     prompt_row(0)
     prompt_column(0)
-    each_window(1, lambda copy: copy.start())
-    prompt_row(1)
 
     width = PER_GROUP * 128
     kk = lax.broadcasted_iota(jnp.int32, (BLOCK, width), 0)
@@ -253,7 +251,7 @@
     lane = lax.rem(lax.broadcasted_iota(jnp.int32, (1, width), 1), BLOCK)
     length = tl_ref[0]
 
-    def unit(g, half, role):
+    def unit(g, half, role, leave=None):
         rho = core if role else other
         dev = chip * 2 + rho
         blk = jnp.where(half == 0, dev, NBLK - 1 - dev)
@@ -267,7 +265,7 @@
         K, V = (jnp.concatenate(
             [prompt[g, s, kv] for s in range(PROMPT)] + [cand[half, g, base + d, kv] for d in range(WINDOW + 1)], 0)
             for kv in range(2))
-        off = [jnp.where(kb_ref[s * NBLK + blk] >= 0, 0.0, FAR).astype(F32) for s in range(SLOTS)]
+        off = [jnp.where(kb_ref[s, 0, blk] >= 0, 0.0, FAR).astype(F32) for s in range(SLOTS)]
         S = dot(K, Q, 1, 1)
         parts, m = [], None
         for s in range(SLOTS):
@@ -288,23 +286,25 @@
         probs = jnp.concatenate(exps, 0) * inv
         low = probs.astype(BF)
         dP = dot(V, G, 1, 1)
-        r = jnp.sum(low.astype(F32) * dP, 0, keepdims=True)
+        r = jnp.sum(probs * dP, 0, keepdims=True)
         dS = (probs * (dP - r)).astype(BF)
         dv = dot(low, G, 1, 0)
         dk = dot(dS, Q, 1, 0) * SCALE
-        dqT = dot(K, dS, 0, 0)
+        for kv, val in ((0, dk), (1, dv)):
+            for s in range(PROMPT):
+                pacc[g, s, kv] = pacc[g, s, kv] + val[s * 128:(s + 1) * 128]
+            for d in range(WINDOW + 1):
+                acc[half, g, base + d, kv] = acc[half, g, base + d, kv] + val[256 + d * 128:384 + d * 128]
+        if leave is not None:
+            leave()
+        dq = dot(dS, K, 0, 0)
         for j in range(PER_GROUP):
-            t = dqT[:, j * 128:(j + 1) * 128].T * SCALE
+            t = dq[j * 128:(j + 1) * 128] * SCALE
             if role:
                 dq_ref[rows, span(core * 2048 + g * 1024 + j * 128, 128)] = t.astype(BF)
             else:
                 dqs[g, rows, j * 128:(j + 1) * 128] = t.astype(BF)
             bsrc[g, j:j + 1, :] = bsrc[g, j:j + 1, :] + jnp.sum(t, 0, keepdims=True)
-        for kv, val in ((0, dk), (1, dv)):
-            for s in range(PROMPT):
-                pacc[g, s, kv] = pacc[g, s, kv] + val[s * 128:(s + 1) * 128]
-            for d in range(WINDOW + 1):
-                acc[half, g, base + d, kv] = acc[half, g, base + d, kv] + val[256 + d * 128:384 + d * 128]
 
     def dq_cross(g, half):
         rows = span(half * BLOCK, BLOCK)
@@ -391,10 +391,8 @@
             zj = lax.rem(z + k, NZ)
             dev = at(zj, x, core)
             rcopy(ps.at[g, :, :, rows16(zj), :], st1.at[g, z], st1_ss.at[g], st1_rs.at[g], dev).start()
-            rcopy(bsrc.at[g], b1.at[g, z], b1_ss.at[g], b1_rs.at[g], dev).start()
         loop(1, NZ, send)
         st1[g, z] = ps[g, :, :, rows16(z), :]
-        b1[g, z] = bsrc[g]
 
     def total_of(ref, g, n):
         total = ref[g, 0].astype(F32)
@@ -413,15 +411,6 @@
         @pl.when(x > 0)
         def _():
             rcopy(st2s.at[g], st2.at[g, x], st2_ss.at[g], st2_rs.at[g], at(z, 0, core)).start()
-        wait_bytes(b1.at[g, pl.ds(0, NZ - 1)], b1_rs.at[g])
-        total = total_of(b1, g, NZ)
-        b2s[g] = total
-        b2[g, x] = total
-
-        def send(k):
-            rcopy(b2s.at[g], b2.at[g, x], b2_ss.at[g], b2_rs.at[g], at(z, lax.rem(x + k, NX), core)).start()
-        loop(1, NX, send)
-
     def to_root(g, root):
         return rcopy(st3s.at[g, root], st3.at[g, core * NZ + z], st3_ss.at[g, root], st3_rs.at[g], root)
 
@@ -438,25 +427,49 @@
                 @pl.when(c != root)
                 def _():
                     to_root(g, root).start()
-        wait_bytes(b2.at[g, pl.ds(0, NX - 1)], b2_rs.at[g])
-        total = total_of(b2, g, NX)
-        b3s[g] = total
-        b3[g, core * NY + y] = total
+    def send_bias():
+        def send(k):
+            rcopy(bsrc, b1.at[z], b1_ss, b1_rs, at(lax.rem(z + k, NZ), x, core)).start()
+        loop(1, NZ, send)
+        b1[z] = bsrc[...]
+
+    def sum_bias(ref, n):
+        total = ref[0]
+        for k in range(1, n):
+            total = total + ref[k]
+        return total
+
+    def bias1():
+        wait_bytes(b1.at[pl.ds(0, NZ - 1)], b1_rs)
+        total = sum_bias(b1, NZ)
+        b2s[...] = total
+        b2[x] = total
+
+        def send(k):
+            rcopy(b2s, b2.at[x], b2_ss, b2_rs, at(z, lax.rem(x + k, NX), core)).start()
+        loop(1, NX, send)
+
+    def bias2():
+        wait_bytes(b2.at[pl.ds(0, NX - 1)], b2_rs)
+        total = sum_bias(b2, NX)
+        b3s[...] = total
+        b3[core * NY + y] = total
 
         def send(k):
             j = lax.rem(core * NY + y + k, 2 * NY)
             pltpu.make_async_remote_copy(
-                src_ref=b3s.at[g], dst_ref=b3.at[g, core * NY + y], send_sem=b3_ss.at[g], recv_sem=b3_rs.at[g],
+                src_ref=b3s, dst_ref=b3.at[core * NY + y], send_sem=b3_ss, recv_sem=b3_rs,
                 device_id={"ctx": chip * 2 + j // NY, "dp": lax.rem(j, NY)}, device_id_type=MESH).start()
         loop(1, 2 * NY, send)
 
-    def step3(g):
-        wait_bytes(b3.at[g, pl.ds(0, 2 * NY - 1)], b3_rs.at[g])
+    def bias3():
+        wait_bytes(b3.at[pl.ds(0, 2 * NY - 1)], b3_rs)
         for r in range(2):
-            total = b3[g, r * NY]
+            total = b3[r * NY]
             for k in range(1, NY):
-                total = total + b3[g, r * NY + k]
-            db_ref[span(r * 16 + g * 8, 8), :] = total * (1.0 / math.sqrt(ROWS))
+                total = total + b3[r * NY + k]
+            for g in range(GROUPS):
+                db_ref[r * 16 + g * 8:r * 16 + g * 8 + 8, :] = total[g] * (1.0 / math.sqrt(ROWS))
 
     def finish(g):
         wait_ret(g)
@@ -501,6 +514,11 @@
             wait_near(g, 0)
             wait_bytes(pieces(prompt, g, NZ - 1), s3_rs.at[g])
 
+        @pl.when(i == 0)
+        def _():
+            scatter_prompt(1)
+            each_window(1, lambda copy: copy.start())
+
         @pl.when(half == 1)
         def _():
             cross(1, g).wait_recv()
@@ -519,42 +537,36 @@
 
         @pl.when(i == 0)
         def _():
+            prompt_row(1)
+
+        @pl.when(i == 2)
+        def _():
+            step1(0)
+
+        def leave():
+            @pl.when(half == 1)
+            def _():
+                send_shared(g)
+
+                @pl.when(chip == CHIPS - 1)
+                def _():
+                    fold_sums(g)
+                    send_low(g)
+                send_up(g)
+
+            @pl.when((half == 0) & (chip < CHIPS - 1))
+            def _():
+                send_low(g)
+        unit(g, half, 1, leave)
+
+        @pl.when(i == 0)
+        def _():
             prompt_column(1)
-
-        @pl.when(i == 2)
-        def _():
-            step1(0)
-        unit(g, half, 1)
-
-        @pl.when(half == 1)
-        def _():
-            send_shared(g)
-
-            @pl.when(chip == CHIPS - 1)
-            def _():
-                fold_sums(g)
-                send_low(g)
-            send_up(g)
-
-        @pl.when((half == 0) & (chip < CHIPS - 1))
-        def _():
-            send_low(g)
 
         @pl.when(i == 2)
         def _():
             step2(0)
     loop(0, 2 * GROUPS, main)
-
-    finish(0)
-    step1(1)
-    finish(1)
-    step2(1)
-    step3(0)
-
-    @pl.when(is_root)
-    def _():
-        loop(0, GROUPS, finish_root)
-    step3(1)
 
     def drain(g):
         for half in range(2):
@@ -580,10 +592,33 @@
             wait_bytes(st2s.at[g], st2_ss.at[g])
         wait_bytes(pieces(prompt, g, NZ - 1), s3_ss.at[g])
         wait_bytes(st1.at[g, pl.ds(0, NZ - 1)], st1_ss.at[g])
-        wait_bytes(b1.at[g, pl.ds(0, NZ - 1)], b1_ss.at[g])
-        wait_bytes(b2.at[g, pl.ds(0, NX - 1)], b2_ss.at[g])
-        wait_bytes(b3.at[g, pl.ds(0, 2 * NY - 1)], b3_ss.at[g])
-    loop(0, GROUPS, drain)
+
+    send_bias()
+    finish(0)
+    step1(1)
+    bias1()
+    drain(0)
+    step2(1)
+    bias2()
+    finish(1)
+
+    @pl.when(is_root)
+    def _():
+        loop(0, GROUPS, finish_root)
+    bias3()
+    drain(1)
+    wait_bytes(b1.at[pl.ds(0, NZ - 1)], b1_ss)
+    wait_bytes(b2.at[pl.ds(0, NX - 1)], b2_ss)
+    wait_bytes(b3.at[pl.ds(0, 2 * NY - 1)], b3_ss)
+
+
+def hand_out(dq, dk, dv, db, dq_out, dk_out, dv_out, db_out, sems):
+    copies = [pltpu.make_async_copy(a, b, sems.at[i])
+              for i, (a, b) in enumerate(((dq, dq_out), (dk, dk_out), (dv, dv_out), (db, db_out)))]
+    for copy in copies:
+        copy.start()
+    for copy in copies:
+        copy.wait()
 
 
 def body(query_in, key_in, value_rows_input, grad_out, query_bias, key_blocks, trace_len):
@@ -616,22 +651,36 @@
             many(G, PROMPT),
             pltpu.VMEM((G, NZ) + part, BF), pltpu.VMEM((G,) + part, BF), pltpu.VMEM((G, NX) + part, BF),
             pltpu.VMEM((G,) + part, BF), pltpu.VMEM((G, 2 * NZ, 2, PIECE, 128), BF),
-            pltpu.VMEM((G, 8, 128), F32), pltpu.VMEM((G, NZ, 8, 128), F32),
-            pltpu.VMEM((G, 8, 128), F32), pltpu.VMEM((G, NX, 8, 128), F32),
-            pltpu.VMEM((G, 8, 128), F32), pltpu.VMEM((G, 2 * NY, 8, 128), F32),
+            pltpu.VMEM((G, 8, 128), F32), pltpu.VMEM((NZ, G, 8, 128), F32),
+            pltpu.VMEM((G, 8, 128), F32), pltpu.VMEM((NX, G, 8, 128), F32),
+            pltpu.VMEM((G, 8, 128), F32), pltpu.VMEM((2 * NY, G, 8, 128), F32),
             dma((G,)), dma((G,)), dma((2, 2, 4)), dma((2, 2, G)),
             dma((G,)), dma((G,)), dma((G,)), dma((G,)), dma((2, G)), dma((2, G)),
             dma((2, G, 2, 2)), dma((2, G, WINDOW)),
             dma((G,)), dma((G, PROMPT)), dma((G,)), dma((G,)), dma((G,)), dma((G,)), dma((G, 2)), dma((G, 2)),
             dma((2, G, WINDOW)), dma((2, G, 2, 2)), dma((G, 2)), dma((2, G)), dma((2, G)),
             dma((G,)), dma((G,)), dma((G,)), dma((G,)), dma((G, PROMPT)), dma((G,)),
-            dma((G,)), dma((G,)), dma((G,)), dma((G,)), dma((G,)), dma((G,)),
+            dma, dma, dma, dma, dma, dma,
         ],
         compiler_params=pltpu.CompilerParams(
             collective_id=0, has_side_effects=True, vmem_limit_bytes=58 * 2**20),
         name="attention",
     )(query_in[0], key_in[0], value_rows_input[0], grad_out[0], query_bias.reshape(32, 128),
-      key_blocks.transpose(2, 0, 1).reshape(-1), trace_len)
+      key_blocks.transpose(2, 0, 1), trace_len)
+    dq, dk, dv, db = pl.pallas_call(
+        hand_out,
+        out_shape=(
+            jax.ShapeDtypeStruct((2 * BLOCK, 4096), BF),
+            jax.ShapeDtypeStruct((2 * BLOCK, 512), BF),
+            jax.ShapeDtypeStruct((2 * BLOCK, 512), BF),
+            jax.ShapeDtypeStruct((32, 128), F32),
+        ),
+        in_specs=[vmem] * 4,
+        out_specs=(any_,) * 4,
+        scratch_shapes=[dma((4,))],
+        compiler_params=pltpu.CompilerParams(has_side_effects=True),
+        name="hand_out",
+    )(*(pltpu.with_memory_space_constraint(a, pltpu.VMEM) for a in (dq, dk, dv, db)))
     return dq[None], dk[None], dv[None], db.reshape(4096)
 
 

time: 77.6 us -> 75.8 us (0.977)
  local copies, waits for them, and re-layouts: 3.96 us -> 0 us
  Pallas kernels: 72.2 us -> 74.4 us
    unnamed x6 -> x0, local copies, waits for them, and re-layouts: 3.36 us -> none
    pallas_call x0 -> x1, Pallas kernels: none -> 1.52 us  [body(): pl.pallas_call(hand_out, out_shape=(jax.ShapeDtypeStruct((2 * BLOCK, 4096...]
where the time goes in v3:
time: 75.8 us; the launch traced here: 75.6 us
  Pallas kernels  74.4 us (98%)
  between operations  1.29 us (2%)
    pallas_call x1, Pallas kernels, body(): pl.pallas_call(kernel, out_shape=(pltpu.VMEM((2 * BLOCK, 4096), BF), pltp...  72.8 us
    pallas_call x1, Pallas kernels, body(): pl.pallas_call(hand_out, out_shape=(jax.ShapeDtypeStruct((2 * BLOCK, 4096...  1.52 us

profile of v3, /device:TPU:1, one launch (start us, length us, event | category | flops | bytes accessed | tf_op | source)
XLA Modules:
  0.0 75.6 jit_solution(1994711757892437921)
XLA Ops:
  1.3 72.8 %attention.1 = (bf16[256,4096]{1,0:T(8,128)(2,1)S(1)}, bf16[256,512]{1,0:T(8,128)(2,1)S(1)}, bf16[256,512]{1,0:T(8,128)(2,1)S(1)}, f32[32,128]{1,0:T(8,128)S(1)}) custom-call(bf16[256,4096]{1,0:T(8,128)(2,1)} %bitcast.10, bf16[256,512]{1,0:T(8,128)(2,1)} %bitcast.12, bf16[256,512]{1,0:T(8,128)(2,1)} %bitcast.13, bf16[256,4096]{1,0:T(8,128)(2,1)} %bitcast.11, ...), custom_call_target="tpu_custom_call" | custom-call | tf_op jit(solution)/shard_map/attention/pallas_call | solution.py:635
  74.1 1.5 %hand_out.1 = (bf16[256,4096]{1,0:T(8,128)(2,1)}, bf16[256,512]{1,0:T(8,128)(2,1)}, bf16[256,512]{1,0:T(8,128)(2,1)}, f32[32,128]{1,0:T(8,128)}) custom-call(bf16[256,4096]{1,0:T(8,128)(2,1)S(1)} %get-tuple-element.12.dq, bf16[256,512]{1,0:T(8,128)(2,1)S(1)} %get-tuple-element.13.dk, bf16[256,512]{1,0:T(8,128)(2,1)S(1)} %get-tuple-element.14.dv, ...), custom_call_target="tpu_custom_call" | custom-call | tf_op jit(solution)/shard_map/hand_out/pallas_call | solution.py:670

commit v4 on v3

--- a/solution.py
+++ b/solution.py
@@ -37,7 +37,7 @@
            qv, gv, stage, prompt, cand, acc, pacc, dqs, ret_s, ret_r, refl_r, sib_s, sib_r,
            ps, st1, st2s, st2, st3s, st3, bsrc, b1, b2s, b2, b3s, b3,
            q_sem, g_sem, kv_sem, own_sem, qx_ss, qx_rs, gx_ss, gx_rs, cx_ss, cx_rs,
-           win_ss, win_rs, s1_ss, s1_rs, s2_ss, s2_rs, s3_ss, s3_rs, dq_ss, dq_rs,
+           win_ss, win_rs, s1_ss, s1_rs, s2_ss, s2_rs, s3_ss, s3_rs, dq_ss, dq_rs, do_sem,
            ret_ss, ret_rs, refl_rs, sib_ss, sib_rs, st1_ss, st1_rs, st2_ss, st2_rs, st3_ss, st3_rs,
            b1_ss, b1_rs, b2_ss, b2_rs, b3_ss, b3_rs):
     c = lax.axis_index("ctx")
@@ -184,33 +184,34 @@
         slot = mine(half)
         return rcopy(stage.at[half, other * 2 + g], cand.at[half, g, slot], cx_ss.at[half, g], cx_rs.at[half, g], sibling)
 
-    def each_window(g, act):
+    def each_near(g, act):
         for r in range(2):
             act(win_low(g, r, 0))
 
             @pl.when(chip >= 1)
             def _():
                 act(win_up(g, r, 0))
-
-            @pl.when(core == 1)
-            def _():
-                act(win_low(g, r, 1))
-
-            @pl.when((core == 0) & (chip >= 2))
-            def _():
-                act(win_up(g, r, 1))
-
-            @pl.when(c == N_CTX - 1)
-            def _():
-                act(win_fold(g, r))
         for half in range(2):
             act(cross(half, g))
         act(q_cross(q_hbm, qv, qx_ss, qx_rs, g))
         act(q_cross(go_hbm, gv, gx_ss, gx_rs, g))
 
-    def wait_near(g, half):
-        cross(half, g).wait_recv()
-        for slot in range(2, NEAR):
+    def each_far(g, act):
+        for r in range(2):
+            @pl.when(core == 1)
+            def _():
+                act(win_low(g, r, 1))
+
+            @pl.when((core == 0) & (chip >= 2))
+            def _():
+                act(win_up(g, r, 1))
+
+            @pl.when(c == N_CTX - 1)
+            def _():
+                act(win_fold(g, r))
+
+    def wait_slots(g, half, slots):
+        for slot in slots:
             rcopy(cand.at[half, g, slot], cand.at[half, g, slot], win_ss.at[0, g, 0, 0], win_rs.at[half, g, slot - 2],
                   sibling).wait_recv()
 
@@ -241,9 +242,10 @@
     def pieces(ref, g, n):
         return ref.at[g, :, :, pl.ds(0, n * PIECE), :]
 
-    each_window(0, lambda copy: copy.start())
+    each_near(0, lambda copy: copy.start())
     prompt_row(0)
     prompt_column(0)
+    each_far(0, lambda copy: copy.start())
 
     width = PER_GROUP * 128
     kk = lax.broadcasted_iota(jnp.int32, (BLOCK, width), 0)
@@ -251,11 +253,12 @@
     lane = lax.rem(lax.broadcasted_iota(jnp.int32, (1, width), 1), BLOCK)
     length = tl_ref[0]
 
-    def unit(g, half, role, leave=None):
-        rho = core if role else other
+    def unit(g, half, turn, leave=None):
+        rho = 1 - turn
+        role = other if turn else core
         dev = chip * 2 + rho
         blk = jnp.where(half == 0, dev, NBLK - 1 - dev)
-        base = jnp.where(half == 0, 1 - rho, rho)
+        base = jnp.where(half == 0, turn, rho)
         rows = span(half * BLOCK, BLOCK)
         bias = bias_ref[span(core * 16 + g * 8, 8), :]
         Q = jnp.concatenate(
@@ -300,16 +303,27 @@
         dq = dot(dS, K, 0, 0)
         for j in range(PER_GROUP):
             t = dq[j * 128:(j + 1) * 128] * SCALE
-            if role:
-                dq_ref[rows, span(core * 2048 + g * 1024 + j * 128, 128)] = t.astype(BF)
-            else:
-                dqs[g, rows, j * 128:(j + 1) * 128] = t.astype(BF)
+            dqs[role, g, rows, j * 128:(j + 1) * 128] = t.astype(BF)
             bsrc[g, j:j + 1, :] = bsrc[g, j:j + 1, :] + jnp.sum(t, 0, keepdims=True)
 
     def dq_cross(g, half):
         rows = span(half * BLOCK, BLOCK)
-        return rcopy(dqs.at[g, rows, :], dq_ref.at[rows, span(core * 2048 + g * 1024, 1024)],
+        return rcopy(dqs.at[0, g, rows, :], dq_ref.at[rows, span(core * 2048 + g * 1024, 1024)],
                      dq_ss.at[g, half], dq_rs.at[g, half], sibling)
+
+    def dq_own(g, half):
+        rows = span(half * BLOCK, BLOCK)
+        return pltpu.make_async_copy(dqs.at[1, g, rows, :], dq_ref.at[rows, span(core * 2048 + g * 1024, 1024)],
+                                     do_sem.at[g, half])
+
+    def dq_leave(g, half, turn):
+        @pl.when(core == turn)
+        def _():
+            dq_cross(g, half).start()
+
+        @pl.when(core != turn)
+        def _():
+            dq_own(g, half).start()
 
     def ret_low(g, e):
         far = 1 if e == 3 else 0
@@ -333,15 +347,24 @@
         act(sib_copy(g, 0))
 
     def each_up(g, act):
-        for e in range(1, WINDOW + 1):
-            @pl.when(chip * 2 + 1 + e < N_CTX)
-            def _():
+        @pl.when(chip < CHIPS - 1)
+        def _():
+            for e in range(1, WINDOW):
                 act(ret_up(g, e))
+        act(sib_copy(g, 1))
+
+    def each_up_far(g, act):
+        @pl.when(chip < CHIPS - 2)
+        def _():
+            act(ret_up(g, WINDOW))
 
         @pl.when(chip == CHIPS - 2)
         def _():
             act(ret_fold(g))
-        act(sib_copy(g, 1))
+
+    def send_up_far(g):
+        ret_s[1, g, 2] = acc[1, g, 4].astype(BF)
+        each_up_far(g, lambda copy: copy.start())
 
     def send_low(g):
         for e in range(WINDOW):
@@ -350,7 +373,7 @@
         each_low(g, lambda copy: copy.start())
 
     def send_up(g):
-        for e in range(WINDOW):
+        for e in range(WINDOW - 1):
             ret_s[1, g, e] = acc[1, g, 2 + e].astype(BF)
         sib_s[1, g] = acc[1, g, other].astype(BF)
         each_up(g, lambda copy: copy.start())
@@ -511,13 +534,15 @@
             q_own(go_hbm, gv, g_sem, g).wait()
             q_cross(q_hbm, qv, qx_ss, qx_rs, g).wait_recv()
             q_cross(go_hbm, gv, gx_ss, gx_rs, g).wait_recv()
-            wait_near(g, 0)
+            cross(0, g).wait_recv()
+            wait_slots(g, 0, (2, 3))
             wait_bytes(pieces(prompt, g, NZ - 1), s3_rs.at[g])
 
         @pl.when(i == 0)
         def _():
             scatter_prompt(1)
-            each_window(1, lambda copy: copy.start())
+            each_near(1, lambda copy: copy.start())
+            each_far(1, lambda copy: copy.start())
 
         @pl.when(half == 1)
         def _():
@@ -525,15 +550,18 @@
 
             @pl.when(chip < CHIPS - 1)
             def _():
-                for slot in range(2, NEAR):
-                    wait_recv(cand.at[1, g, slot], win_rs.at[1, g, slot - 2])
+                wait_slots(g, 1, range(2, NEAR))
 
             @pl.when(chip == CHIPS - 1)
             def _():
                 for slot in range(2, NEAR):
                     cand[1, g, slot] = cand[0, g, slot - 2]
         unit(g, half, 0)
-        dq_cross(g, half).start()
+
+        @pl.when(half == 1)
+        def _():
+            send_up_far(g)
+        dq_leave(g, half, 0)
 
         @pl.when(i == 0)
         def _():
@@ -557,7 +585,12 @@
             @pl.when((half == 0) & (chip < CHIPS - 1))
             def _():
                 send_low(g)
+
+        @pl.when(half == 0)
+        def _():
+            wait_slots(g, 0, (4,))
         unit(g, half, 1, leave)
+        dq_leave(g, half, 1)
 
         @pl.when(i == 0)
         def _():
@@ -571,9 +604,12 @@
     def drain(g):
         for half in range(2):
             dq_cross(g, half).wait()
-        each_window(g, lambda copy: copy.wait_send())
+            dq_own(g, half).wait()
+        each_near(g, lambda copy: copy.wait_send())
+        each_far(g, lambda copy: copy.wait_send())
         each_low(g, lambda copy: copy.wait_send())
         each_up(g, lambda copy: copy.wait_send())
+        each_up_far(g, lambda copy: copy.wait_send())
 
         @pl.when(is_root)
         def _():
@@ -646,7 +682,7 @@
             pltpu.VMEM((2, G, 2 * BLOCK, 1024), BF), pltpu.VMEM((2, G, 2 * BLOCK, 1024), BF),
             many(2, 4), many(G, PROMPT), many(2, G, NEAR),
             pltpu.VMEM((2, G, NEAR) + tile, F32), pltpu.VMEM((G, PROMPT) + tile, F32),
-            pltpu.VMEM((G, 2 * BLOCK, 1024), BF),
+            pltpu.VMEM((2, G, 2 * BLOCK, 1024), BF),
             many(2, G, WINDOW), many(2, G, 2, 2), many(G, 2), many(2, G), many(2, G),
             many(G, PROMPT),
             pltpu.VMEM((G, NZ) + part, BF), pltpu.VMEM((G,) + part, BF), pltpu.VMEM((G, NX) + part, BF),
@@ -657,7 +693,7 @@
             dma((G,)), dma((G,)), dma((2, 2, 4)), dma((2, 2, G)),
             dma((G,)), dma((G,)), dma((G,)), dma((G,)), dma((2, G)), dma((2, G)),
             dma((2, G, 2, 2)), dma((2, G, WINDOW)),
-            dma((G,)), dma((G, PROMPT)), dma((G,)), dma((G,)), dma((G,)), dma((G,)), dma((G, 2)), dma((G, 2)),
+            dma((G,)), dma((G, PROMPT)), dma((G,)), dma((G,)), dma((G,)), dma((G,)), dma((G, 2)), dma((G, 2)), dma((G, 2)),
             dma((2, G, WINDOW)), dma((2, G, 2, 2)), dma((G, 2)), dma((2, G)), dma((2, G)),
             dma((G,)), dma((G,)), dma((G,)), dma((G,)), dma((G, PROMPT)), dma((G,)),
             dma, dma, dma, dma, dma, dma,

time: 75.8 us -> 76.3 us (level)
  no operation moved by 1% of the time
where the time goes in v4:
time: 76.3 us; the launch traced here: 76.1 us
  Pallas kernels  74.8 us (98%)
  between operations  1.29 us (2%)
    pallas_call x1, Pallas kernels, body(): pl.pallas_call(kernel, out_shape=(pltpu.VMEM((2 * BLOCK, 4096), BF), pltp...  73.3 us

profile of v4, /device:TPU:1, one launch (start us, length us, event | category | flops | bytes accessed | tf_op | source)
XLA Modules:
  0.0 76.1 jit_solution(6474725614799848812)
XLA Ops:
  1.3 73.3 %attention.1 = (bf16[256,4096]{1,0:T(8,128)(2,1)S(1)}, bf16[256,512]{1,0:T(8,128)(2,1)S(1)}, bf16[256,512]{1,0:T(8,128)(2,1)S(1)}, f32[32,128]{1,0:T(8,128)S(1)}) custom-call(bf16[256,4096]{1,0:T(8,128)(2,1)} %bitcast.10, bf16[256,512]{1,0:T(8,128)(2,1)} %bitcast.12, bf16[256,512]{1,0:T(8,128)(2,1)} %bitcast.13, bf16[256,4096]{1,0:T(8,128)(2,1)} %bitcast.11, ...), custom_call_target="tpu_custom_call" | custom-call | tf_op jit(solution)/shard_map/attention/pallas_call | solution.py:671
  74.6 1.5 %hand_out.1 = (bf16[256,4096]{1,0:T(8,128)(2,1)}, bf16[256,512]{1,0:T(8,128)(2,1)}, bf16[256,512]{1,0:T(8,128)(2,1)}, f32[32,128]{1,0:T(8,128)}) custom-call(bf16[256,4096]{1,0:T(8,128)(2,1)S(1)} %get-tuple-element.12.dq, bf16[256,512]{1,0:T(8,128)(2,1)S(1)} %get-tuple-element.13.dk, bf16[256,512]{1,0:T(8,128)(2,1)S(1)} %get-tuple-element.14.dv, ...), custom_call_target="tpu_custom_call" | custom-call | tf_op jit(solution)/shard_map/hand_out/pallas_call | solution.py:706

commit v5 on v3

--- a/solution.py
+++ b/solution.py
@@ -66,6 +66,10 @@
             return carry
         lax.fori_loop(lo, hi, step, 0)
 
+    def each(lo, hi, f):
+        for i in range(lo, hi):
+            f(i)
+
     def span(start, size):
         return pl.ds(pl.multiple_of(start, size), size)
 
@@ -227,7 +231,7 @@
 
             def send(k):
                 rcopy(prompt_piece(g), prompt_piece(g), s2_ss.at[g], s2_rs.at[g], at(z, k, core)).start()
-            loop(1, NX, send)
+            each(1, NX, send)
 
     def prompt_column(g):
         @pl.when(x > 0)
@@ -236,7 +240,7 @@
 
         def send(k):
             rcopy(prompt_piece(g), prompt_piece(g), s3_ss.at[g], s3_rs.at[g], at(lax.rem(z + k, NZ), x, core)).start()
-        loop(1, NZ, send)
+        each(1, NZ, send)
 
     def pieces(ref, g, n):
         return ref.at[g, :, :, pl.ds(0, n * PIECE), :]
@@ -391,7 +395,7 @@
             zj = lax.rem(z + k, NZ)
             dev = at(zj, x, core)
             rcopy(ps.at[g, :, :, rows16(zj), :], st1.at[g, z], st1_ss.at[g], st1_rs.at[g], dev).start()
-        loop(1, NZ, send)
+        each(1, NZ, send)
         st1[g, z] = ps[g, :, :, rows16(z), :]
 
     def total_of(ref, g, n):
@@ -430,7 +434,7 @@
     def send_bias():
         def send(k):
             rcopy(bsrc, b1.at[z], b1_ss, b1_rs, at(lax.rem(z + k, NZ), x, core)).start()
-        loop(1, NZ, send)
+        each(1, NZ, send)
         b1[z] = bsrc[...]
 
     def sum_bias(ref, n):
@@ -447,7 +451,7 @@
 
         def send(k):
             rcopy(b2s, b2.at[x], b2_ss, b2_rs, at(z, lax.rem(x + k, NX), core)).start()
-        loop(1, NX, send)
+        each(1, NX, send)
 
     def bias2():
         wait_bytes(b2.at[pl.ds(0, NX - 1)], b2_rs)
@@ -460,7 +464,7 @@
             pltpu.make_async_remote_copy(
                 src_ref=b3s, dst_ref=b3.at[core * NY + y], send_sem=b3_ss, recv_sem=b3_rs,
                 device_id={"ctx": chip * 2 + j // NY, "dp": lax.rem(j, NY)}, device_id_type=MESH).start()
-        loop(1, 2 * NY, send)
+        each(1, 2 * NY, send)
 
     def bias3():
         wait_bytes(b3.at[pl.ds(0, 2 * NY - 1)], b3_rs)
@@ -595,20 +599,24 @@
 
     send_bias()
     finish(0)
+
+    @pl.when(is_root)
+    def _():
+        finish_root(0)
     step1(1)
     bias1()
     drain(0)
     step2(1)
     bias2()
     finish(1)
-
-    @pl.when(is_root)
-    def _():
-        loop(0, GROUPS, finish_root)
-    bias3()
     drain(1)
     wait_bytes(b1.at[pl.ds(0, NZ - 1)], b1_ss)
     wait_bytes(b2.at[pl.ds(0, NX - 1)], b2_ss)
+
+    @pl.when(is_root)
+    def _():
+        finish_root(1)
+    bias3()
     wait_bytes(b3.at[pl.ds(0, 2 * NY - 1)], b3_ss)
 
 

time: 75.8 us -> 75.9 us (level)
  no operation moved by 1% of the time
where the time goes in v5:
time: 75.9 us; the launch traced here: 75.7 us
  Pallas kernels  74.5 us (98%)
  between operations  1.29 us (2%)
    pallas_call x1, Pallas kernels, body(): pl.pallas_call(kernel, out_shape=(pltpu.VMEM((2 * BLOCK, 4096), BF), pltp...  72.9 us
    pallas_call x1, Pallas kernels, body(): pl.pallas_call(hand_out, out_shape=(jax.ShapeDtypeStruct((2 * BLOCK, 4096...  1.52 us

profile of v5, /device:TPU:1, one launch (start us, length us, event | category | flops | bytes accessed | tf_op | source)
XLA Modules:
  0.0 75.7 jit_solution(1264704179774177470)
XLA Ops:
  1.3 72.9 %attention.1 = (bf16[256,4096]{1,0:T(8,128)(2,1)S(1)}, bf16[256,512]{1,0:T(8,128)(2,1)S(1)}, bf16[256,512]{1,0:T(8,128)(2,1)S(1)}, f32[32,128]{1,0:T(8,128)S(1)}) custom-call(bf16[256,4096]{1,0:T(8,128)(2,1)} %bitcast.10, bf16[256,512]{1,0:T(8,128)(2,1)} %bitcast.12, bf16[256,512]{1,0:T(8,128)(2,1)} %bitcast.13, bf16[256,4096]{1,0:T(8,128)(2,1)} %bitcast.11, ...), custom_call_target="tpu_custom_call" | custom-call | tf_op jit(solution)/shard_map/attention/pallas_call | solution.py:643
  74.2 1.5 %hand_out.1 = (bf16[256,4096]{1,0:T(8,128)(2,1)}, bf16[256,512]{1,0:T(8,128)(2,1)}, bf16[256,512]{1,0:T(8,128)(2,1)}, f32[32,128]{1,0:T(8,128)}) custom-call(bf16[256,4096]{1,0:T(8,128)(2,1)S(1)} %get-tuple-element.12.dq, bf16[256,512]{1,0:T(8,128)(2,1)S(1)} %get-tuple-element.13.dk, bf16[256,512]{1,0:T(8,128)(2,1)S(1)} %get-tuple-element.14.dv, ...), custom_call_target="tpu_custom_call" | custom-call | tf_op jit(solution)/shard_map/hand_out/pallas_call | solution.py:678

commit v6 on v5

--- a/solution.py
+++ b/solution.py
@@ -96,7 +96,6 @@
         for half in range(2):
             for kv in range(2):
                 kv_stage(half, kv, h).start()
-    loop(0, 4, start_stage)
 
     def start_own(g):
         for half in range(2):
@@ -104,7 +103,12 @@
                 kv_own(half, kv, g).start()
         q_own(q_hbm, qv, q_sem, g).start()
         q_own(go_hbm, gv, g_sem, g).start()
-    loop(0, GROUPS, start_own)
+
+    def zero_landing(g):
+        for half in range(2):
+            ret_r[half, g] = jnp.zeros((2, 2, 2, BLOCK, 128), BF)
+        refl_r[g] = jnp.zeros((2, 2, BLOCK, 128), BF)
+    loop(0, GROUPS, zero_landing)
 
     barrier = pltpu.get_barrier_semaphore()
 
@@ -137,11 +141,12 @@
         greet(sibling, yy)
     loop(1, NY, greet_y)
 
+    loop(0, 4, start_stage)
+    loop(0, GROUPS, start_own)
+
     def zero(g):
         for half in range(2):
-            ret_r[half, g] = jnp.zeros((2, 2, 2, BLOCK, 128), BF)
             acc[half, g] = jnp.zeros((NEAR, 2, BLOCK, 128), F32)
-        refl_r[g] = jnp.zeros((2, 2, BLOCK, 128), BF)
         pacc[g] = jnp.zeros((PROMPT, 2, BLOCK, 128), F32)
         bsrc[g] = jnp.zeros((8, 128), F32)
     loop(0, GROUPS, zero)

time: 75.9 us -> 76 us (level)
  no operation moved by 1% of the time
where the time goes in v6:
time: 76 us; the launch traced here: 75.8 us
  Pallas kernels  74.5 us (98%)
  between operations  1.29 us (2%)
    pallas_call x1, Pallas kernels, body(): pl.pallas_call(kernel, out_shape=(pltpu.VMEM((2 * BLOCK, 4096), BF), pltp...  73 us

profile of v6, /device:TPU:1, one launch (start us, length us, event | category | flops | bytes accessed | tf_op | source)
XLA Modules:
  0.0 75.8 jit_solution(5881424449742675912)
XLA Ops:
  1.3 73.0 %attention.1 = (bf16[256,4096]{1,0:T(8,128)(2,1)S(1)}, bf16[256,512]{1,0:T(8,128)(2,1)S(1)}, bf16[256,512]{1,0:T(8,128)(2,1)S(1)}, f32[32,128]{1,0:T(8,128)S(1)}) custom-call(bf16[256,4096]{1,0:T(8,128)(2,1)} %bitcast.10, bf16[256,512]{1,0:T(8,128)(2,1)} %bitcast.12, bf16[256,512]{1,0:T(8,128)(2,1)} %bitcast.13, bf16[256,4096]{1,0:T(8,128)(2,1)} %bitcast.11, ...), custom_call_target="tpu_custom_call" | custom-call | tf_op jit(solution)/shard_map/attention/pallas_call | solution.py:648
  74.3 1.5 %hand_out.1 = (bf16[256,4096]{1,0:T(8,128)(2,1)}, bf16[256,512]{1,0:T(8,128)(2,1)}, bf16[256,512]{1,0:T(8,128)(2,1)}, f32[32,128]{1,0:T(8,128)}) custom-call(bf16[256,4096]{1,0:T(8,128)(2,1)S(1)} %get-tuple-element.12.dq, bf16[256,512]{1,0:T(8,128)(2,1)S(1)} %get-tuple-element.13.dk, bf16[256,512]{1,0:T(8,128)(2,1)S(1)} %get-tuple-element.14.dv, ...), custom_call_target="tpu_custom_call" | custom-call | tf_op jit(solution)/shard_map/hand_out/pallas_call | solution.py:683
